TPU v7x, 32 devices: a whole 2x2x4 slice. The times are simulated.
32 devices in a mesh: grp: 8 (over y, x, core), dom: 4 (over z).
Axes of the slice: x: 2, y: 2, z: 4, core: 2. Of those that a mesh axis runs over, the one named last changes fastest.
Arguments:
- positions: float32 [5632, 1024], P('grp', 'dom'), may hold values from 0 to 32
- energies: float32 [5632, 1024], P('grp', 'dom'), may hold values from -6 to 6
- bucket: int32 [5632], P('grp'), may hold values from 0 to 2047, as said below
- impedance: float32 [3, 2, 64, 32, 256], P(None, None, 'dom', 'grp'), may hold values from -6 to 6
- history: float32 [2, 2, 64, 32, 256], P(None, None, 'dom', 'grp'), may hold values from -1.8 to 1.8
Outputs:
- positions_out: float32 [5632, 1024], P('grp', 'dom')
- energies_out: float32 [5632, 1024], P('grp', 'dom')
- spectrum: float32 [2, 64, 32, 256], P(None, 'dom', 'grp')
Inputs may be any that keep to these rules, and one draw needn't show every extreme that they name: Within one train group no two bunches share a bucket; the first bunch of each group sits in bucket 0 and its last bunch in bucket 2048 - 1.
All inputs are finite; a program needn't handle non-finite values.
Results may differ from a plain program's by a relative error of at most 0.00013.
Values sent between devices are 32-bit elements; how exact they have to be, the bound alone decides.
A program may use at most 64 MiB of HBM per device.

v0:
```python
import math

import jax
import jax.numpy as jnp
from jax import lax
from jax.sharding import PartitionSpec as P

BINS = 32
N3 = 256
R1 = 8
R2 = 8
HIST = 2
BUNCH_GRP = 704
P_DEV = 256


highest = lax.Precision.HIGHEST
two_pi = 2.0 * math.pi


def kernel_table(places):
    centers = jnp.arange(BINS, dtype=jnp.float32) + 0.5
    offset = places[:, None, :] - centers[None, :, None]
    return jnp.exp(-0.5 * offset * offset)


def dft_tables(length):
    series = jnp.arange(length, dtype=jnp.int32)
    windings = series[:, None] * series[None, :] % length
    angles = windings.astype(jnp.float32) * (two_pi / length)
    return (jnp.cos(angles), jnp.sin(angles))


def rotation(windings, modulus):
    angles = (windings % modulus).astype(jnp.float32) * (two_pi / modulus)
    return (jnp.cos(angles), jnp.sin(angles))


def contract(pattern, operand, matrix):
    return jnp.einsum(pattern, operand, matrix, precision=highest)


def on_device(positions, energies, bucket, impedance, history):
    groups = lax.axis_size("grp")
    domains = lax.axis_size("dom")
    group_index = lax.axis_index("grp")
    domain_index = lax.axis_index("dom")
    first_len = R1 * groups
    second_len = R2 * domains
    cycle_len = first_len * second_len * N3
    plane_len = second_len * N3
    depth_len = N3 // groups
    first_part = first_len // domains
    second_part = second_len // groups
    per_row = N3 // BINS
    row_buckets = second_len * per_row
    own_rows = R2 * per_row
    blocks = BUNCH_GRP // 16
    place_blocks = positions.reshape(blocks, 16, P_DEV)

    def partial_profile(place_block):
        return jnp.sum(kernel_table(place_block), axis=2) / float(P_DEV * domains)

    partial_value = lax.map(partial_profile, place_blocks).reshape(BUNCH_GRP, BINS)
    first_row = bucket // row_buckets
    within = bucket % row_buckets
    owner_dom = within // own_rows
    owned_here = owner_dom == domain_index
    local_row = jnp.where(owned_here, within - owner_dom * own_rows, 0)
    totals = lax.psum(partial_value, "dom")
    kept_rows = jnp.where(owned_here[:, None], totals, 0.0)
    line_slab = jnp.zeros((R1, own_rows, BINS), jnp.float32).at[first_row, local_row].add(kept_rows)
    density = line_slab.reshape(R1, R2, N3)
    cos_first, sin_first = dft_tables(first_len)
    cos_second, sin_second = dft_tables(second_len)
    cos_third, sin_third = dft_tables(N3)
    received = lax.all_to_all(density, "grp", split_axis=2, concat_axis=0, tiled=True)
    real_out = contract("nab,kn->abk", received, cos_first)
    imag_out = -contract("nab,kn->abk", received, sin_first)
    rows_real = real_out
    rows_imag = imag_out
    second_global = domain_index * R2 + jnp.arange(R2, dtype=jnp.int32)
    depth_global = group_index * depth_len + jnp.arange(depth_len, dtype=jnp.int32)
    first_freq = jnp.arange(first_len, dtype=jnp.int32)
    cos_turn, sin_turn = rotation(
        first_freq[None, None, :]
        * (second_global[:, None, None] * N3 + depth_global[None, :, None]),
        cycle_len,
    )
    twist_real = rows_real * cos_turn + rows_imag * sin_turn
    twist_imag = rows_imag * cos_turn - rows_real * sin_turn
    part_real = lax.all_to_all(twist_real, "dom", split_axis=2, concat_axis=0, tiled=True)
    part_imag = lax.all_to_all(twist_imag, "dom", split_axis=2, concat_axis=0, tiled=True)
    real_out = contract("nbk,mn->bkm", part_real, cos_second) + contract(
        "nbk,mn->bkm", part_imag, sin_second
    )
    imag_out = contract("nbk,mn->bkm", part_imag, cos_second) - contract(
        "nbk,mn->bkm", part_real, sin_second
    )
    cols_real = real_out
    cols_imag = imag_out
    second_freq = jnp.arange(second_len, dtype=jnp.int32)
    cos_turn, sin_turn = rotation(
        depth_global[:, None, None] * second_freq[None, None, :], plane_len
    )
    turned_real = cols_real * cos_turn + cols_imag * sin_turn
    turned_imag = cols_imag * cos_turn - cols_real * sin_turn
    part_real = lax.all_to_all(turned_real, "grp", split_axis=2, concat_axis=0, tiled=True)
    part_imag = lax.all_to_all(turned_imag, "grp", split_axis=2, concat_axis=0, tiled=True)
    real_out = contract("nac,kn->ack", part_real, cos_third) + contract(
        "nac,kn->ack", part_imag, sin_third
    )
    imag_out = contract("nac,kn->ack", part_imag, cos_third) - contract(
        "nac,kn->ack", part_real, sin_third
    )
    full_real = real_out
    full_imag = imag_out
    norm_factor = 1.0 / math.sqrt(BUNCH_GRP * groups)
    spec_real = full_real * norm_factor
    spec_imag = full_imag * norm_factor
    spectrum = jnp.stack([spec_real, spec_imag])
    volt_real = impedance[0, 0] * spec_real - impedance[0, 1] * spec_imag
    volt_imag = impedance[0, 0] * spec_imag + impedance[0, 1] * spec_real
    for earlier in range(HIST):
        past_real = history[earlier, 0]
        past_imag = history[earlier, 1]
        volt_real = (
            volt_real
            + impedance[earlier + 1, 0] * past_real
            - impedance[earlier + 1, 1] * past_imag
        )
        volt_imag = (
            volt_imag
            + impedance[earlier + 1, 0] * past_imag
            + impedance[earlier + 1, 1] * past_real
        )
    back_real = contract("ack,nk->acn", volt_real, cos_third) - contract(
        "ack,nk->acn", volt_imag, sin_third
    )
    back_imag = contract("ack,nk->acn", volt_real, sin_third) + contract(
        "ack,nk->acn", volt_imag, cos_third
    )
    second_own = group_index * second_part + jnp.arange(second_part, dtype=jnp.int32)
    depth_all = jnp.arange(N3, dtype=jnp.int32)
    cos_turn, sin_turn = rotation(second_own[None, :, None] * depth_all[None, None, :], plane_len)
    lift_real = back_real * cos_turn - back_imag * sin_turn
    lift_imag = back_real * sin_turn + back_imag * cos_turn
    part_real = lax.all_to_all(lift_real, "grp", split_axis=2, concat_axis=1, tiled=True)
    part_imag = lax.all_to_all(lift_imag, "grp", split_axis=2, concat_axis=1, tiled=True)
    real_out = contract("akb,nk->anb", part_real, cos_second) - contract(
        "akb,nk->anb", part_imag, sin_second
    )
    imag_out = contract("akb,nk->anb", part_real, sin_second) + contract(
        "akb,nk->anb", part_imag, cos_second
    )
    first_own = domain_index * first_part + jnp.arange(first_part, dtype=jnp.int32)
    cos_turn, sin_turn = rotation(
        first_own[:, None, None] * (second_freq[None, :, None] * N3 + depth_global[None, None, :]),
        cycle_len,
    )
    spin_real = real_out * cos_turn - imag_out * sin_turn
    spin_imag = real_out * sin_turn + imag_out * cos_turn
    inverse_factor = 1.0 / math.sqrt(cycle_len)
    part_real = lax.all_to_all(spin_real, "dom", split_axis=1, concat_axis=0, tiled=True)
    part_imag = lax.all_to_all(spin_imag, "dom", split_axis=1, concat_axis=0, tiled=True)
    summed = contract("kab,nk->nab", part_real, cos_first) - contract(
        "kab,nk->nab", part_imag, sin_first
    )
    volt_part = summed * inverse_factor
    volt_slab = lax.all_to_all(volt_part, "grp", split_axis=0, concat_axis=2, tiled=True).reshape(
        R1, own_rows, BINS
    )
    volt_group = lax.all_gather(volt_slab, "dom", axis=1, tiled=True)
    volt_rows = volt_group[first_row, within]

    def kick_block(inputs):
        place_block, volt_block = inputs
        table_block = kernel_table(place_block)
        weighted = jnp.einsum("bjp,bj->bp", table_block, volt_block, precision=highest)
        return weighted / jnp.sum(table_block, axis=1)

    kick_volts = lax.map(kick_block, (place_blocks, volt_rows.reshape(blocks, 16, BINS))).reshape(
        BUNCH_GRP, P_DEV
    )
    energies_out = energies - 0.5 * jnp.sin(two_pi * (positions - 0.5 * BINS) / BINS) - kick_volts
    positions_out = positions + 0.25 * energies_out
    return (positions_out, energies_out, spectrum)


def solution(mesh):
    placed = (
        P("grp", "dom"),
        P("grp", "dom"),
        P("grp"),
        P(None, None, "dom", "grp", None),
        P(None, None, "dom", "grp", None),
    )
    return jax.shard_map(
        on_device,
        mesh=mesh,
        in_specs=placed,
        out_specs=(P("grp", "dom"), P("grp", "dom"), P(None, "dom", "grp", None)),
        check_vma=False,
    )
```

profile of v0, /device:TPU:0, one launch (start us, length us, event | category | flops | bytes accessed | tf_op | source)
XLA Modules:
  0.0 346.1 jit_solution(17605901067044137029)
XLA Ops:
  7.2 69.8 %while.20 = (s32[]{:T(128)}, f32[44,16,32]{2,1,0:T(8,128)}, f32[44,16,256]{2,1,0:T(8,128)}, s32[]{:T(128)}) while((s32[]{:T(128)}, f32[44,16,32]{2,1,0:T(8,128)}, f32[44,16,256]{2,1,0:T(8,128)}, s32[]{:T(128)}) %tuple.73), condition=%wide.region_2.3_spmd, body=%wide.region_0.2_spmd.sunk | while | flops 524322 | bytes 62265 | solution.py:64
  78.2 38.2 %all-reduce.2.cloned.1.call-done = f32[704,32]{1,0:T(8,128)} async-done(((f32[704,32]{1,0:T(8,128)}), f32[704,32]{1,0:T(8,128)}) %all-reduce.2.cloned.1.call-update) | async-done | bytes 90128 | tf_op jit(solution)/shard_map/psum | solution.py:70
  117.6 36.0 %scatter_fusion = f32[8,64,32]{2,1,0:T(8,128)S(1)} fusion(f32[8,64,32]{2,1,0:T(8,128)S(1)} %broadcast_in_dim.34, s32[704]{0:T(1024)S(1)} %get-tuple-element.57, f32[704,32]{1,0:T(8,128)S(1)} %broadcast_select_fusion), kind=kCustom, calls=%fused_computation.1 | custom fusion | flops 22528 | bytes 275968 | tf_op jit(solution)/shard_map/scatter-add | solution.py:72
  155.3 3.7 %all-to-all-start = ((f32[8,1,2048]{2,1,0:T(1,128)}), f32[8,1,2048]{2,1,0:T(1,128)S(1)}, u32[]{:S(2)}, u32[]{:S(2)}) async-start(f32[8,1,2048]{2,1,0:T(1,128)} %reshape.318), calls=%async_computation | async-start | bytes 131072 | tf_op jit(solution)/shard_map/all_to_all | solution.py:77
  159.0 4.9 %all-to-all-done = f32[8,1,2048]{2,1,0:T(1,128)S(1)} async-done(((f32[8,1,2048]{2,1,0:T(1,128)}), f32[8,1,2048]{2,1,0:T(1,128)S(1)}, u32[]{:S(2)}, u32[]{:S(2)}) %all-to-all-start) | async-done | bytes 65568 | tf_op jit(solution)/shard_map/all_to_all | solution.py:77
  168.6 3.5 %all-to-all-start.1 = ((f32[4,1,4096]{2,1,0:T(1,128)}), f32[4,1,4096]{2,1,0:T(1,128)S(1)}, u32[]{:S(2)}, u32[]{:S(2)}) async-start(f32[4,1,4096]{2,1,0:T(1,128)} %reshape.320), calls=%async_computation.1 | async-start | bytes 131072 | tf_op jit(solution)/shard_map/all_to_all | solution.py:92
  173.0 4.8 %all-to-all-done.1 = f32[4,1,4096]{2,1,0:T(1,128)S(1)} async-done(((f32[4,1,4096]{2,1,0:T(1,128)}), f32[4,1,4096]{2,1,0:T(1,128)S(1)}, u32[]{:S(2)}, u32[]{:S(2)}) %all-to-all-start.1) | async-done | bytes 65568 | tf_op jit(solution)/shard_map/all_to_all | solution.py:92
  177.8 3.3 all-to-all-start.2
  182.8 4.0 %all-to-all-done.2 = f32[4,1,4096]{2,1,0:T(1,128)S(1)} async-done(((f32[4,1,4096]{2,1,0:T(1,128)}), f32[4,1,4096]{2,1,0:T(1,128)S(1)}, u32[]{:S(2)}, u32[]{:S(2)}) %all-to-all-start.2) | async-done | bytes 65568 | tf_op jit(solution)/shard_map/all_to_all | solution.py:93
  190.4 3.4 all-to-all-start.4
  194.8 3.9 %all-to-all-done.4 = f32[8,1,2048]{2,1,0:T(1,128)S(1)} async-done(((f32[8,1,2048]{2,1,0:T(1,128)}), f32[8,1,2048]{2,1,0:T(1,128)S(1)}, u32[]{:S(2)}, u32[]{:S(2)}) %all-to-all-start.4) | async-done | bytes 65568 | tf_op jit(solution)/shard_map/all_to_all | solution.py:109
  198.7 3.5 %all-to-all-start.3 = ((f32[8,1,2048]{2,1,0:T(1,128)}), f32[8,1,2048]{2,1,0:T(1,128)S(1)}, u32[]{:S(2)}, u32[]{:S(2)}) async-start(f32[8,1,2048]{2,1,0:T(1,128)} %reshape.326), calls=%async_computation.3 | async-start | bytes 131072 | tf_op jit(solution)/shard_map/all_to_all | solution.py:108
  204.8 2.2 all-to-all-done.3
  209.6 1.3 fusion.12
  210.9 1.4 bitcast_add_fusion
  213.6 1.3 fusion.20
  214.9 1.3 convolution_subtract_fusion.2
  218.9 3.6 %all-to-all-start.5 = ((f32[8,1,2048]{2,1,0:T(1,128)}), f32[8,1,2048]{2,1,0:T(1,128)S(1)}, u32[]{:S(2)}, u32[]{:S(2)}) async-start(f32[8,1,2048]{2,1,0:T(1,128)} %reshape.328), calls=%async_computation.5 | async-start | bytes 131072 | tf_op jit(solution)/shard_map/all_to_all | solution.py:148
  223.8 3.4 all-to-all-done.5
  227.2 3.4 all-to-all-start.6
  233.0 2.5 all-to-all-done.6
  237.5 1.4 multiply_add_fusion.1
  239.9 3.3 all-to-all-start.8
  244.1 4.7 %all-to-all-done.8 = f32[4,1,4096]{2,1,0:T(1,128)S(1)} async-done(((f32[4,1,4096]{2,1,0:T(1,128)}), f32[4,1,4096]{2,1,0:T(1,128)S(1)}, u32[]{:S(2)}, u32[]{:S(2)}) %all-to-all-start.8) | async-done | bytes 65568 | tf_op jit(solution)/shard_map/all_to_all | solution.py:165
  248.9 3.3 all-to-all-start.7
  253.8 4.1 %all-to-all-done.7 = f32[4,1,4096]{2,1,0:T(1,128)S(1)} async-done(((f32[4,1,4096]{2,1,0:T(1,128)}), f32[4,1,4096]{2,1,0:T(1,128)S(1)}, u32[]{:S(2)}, u32[]{:S(2)}) %all-to-all-start.7) | async-done | bytes 65568 | tf_op jit(solution)/shard_map/all_to_all | solution.py:164
  260.5 3.4 all-to-all-start.9
  264.6 4.2 %all-to-all-done.9 = f32[8,1,2048]{2,1,0:T(1,128)S(1)} async-done(((f32[8,1,2048]{2,1,0:T(1,128)}), f32[8,1,2048]{2,1,0:T(1,128)S(1)}, u32[]{:S(2)}, u32[]{:S(2)}) %all-to-all-start.9) | async-done | bytes 65568 | tf_op jit(solution)/shard_map/all_to_all | solution.py:170
  269.9 21.4 %all_gather.3 = f32[8,256,32]{2,1,0:T(8,128)S(1)} all-gather(f32[8,64,32]{2,1,0:T(8,128)S(1)} %bitcast.245), channel_id=1, replica_groups=mesh['grp'=8,'dom'=4] {'dom'}, dimensions={1}, use_global_device_ids=true | all-gather | bytes 327680 | tf_op jit(solution)/shard_map/all_gather | solution.py:173
  291.4 7.7 %gather_fusion = f32[704,32]{1,0:T(8,128)S(1)} fusion(f32[8,256,32]{2,1,0:T(8,128)S(1)} %all_gather.3, s32[704]{0:T(1024)S(1)} %get-tuple-element.56), kind=kCustom, calls=%fused_computation | custom fusion | bytes 185856 | tf_op jit(solution)/shard_map/gather | solution.py:174
  299.1 36.7 %while.21 = (s32[]{:T(128)}, f32[44,16,256]{2,1,0:T(8,128)S(1)}, f32[44,16,256]{2,1,0:T(8,128)S(1)}, f32[44,16,32]{2,1,0:T(8,128)S(1)}, s32[]{:T(128)}) while((s32[]{:T(128)}, f32[44,16,256]{2,1,0:T(8,128)S(1)}, f32[44,16,256]{2,1,0:T(8,128)S(1)}, f32[44,16,32]{2,1,0:T(8,128)S(1)}, s32[]{:T(128)}) %tuple.75), condition=%wide.region_7.8_spmd, body=%wide.region_5.7_spmd.sunk | while | flops 2490402 | bytes 154057 | solution.py:182
  335.9 3.4 multiply_add_fusion
  (544 shorter events, 142.5 us)
Async XLA Ops:
  7.2 109.3 %all-reduce.2.cloned.1.call-start = ((), (), s32[]{:S(2)}) async-start(), calls=%async_computation.10 | async-start | bytes 720896 | tf_op jit(solution)/shard_map/psum | solution.py:70
  7.2 69.9 %copy-start.4 = (s32[704]{0:T(1024)S(1)}, s32[704]{0:T(1024)}, u32[]{:S(2)}) copy-start(s32[704]{0:T(1024)} %param.11) | copy-start | bytes 8452
  7.2 70.1 %copy-start.3 = (f32[2,2,16,4,256]{4,3,2,1,0:T(4,128)S(1)}, f32[2,2,16,4,256]{4,3,2,1,0:T(4,128)}, u32[]{:S(2)}) copy-start(f32[2,2,16,4,256]{4,3,2,1,0:T(4,128)} %param.13) | copy-start | bytes 786436
  77.0 1.0 copy-start.2
  155.3 8.7 %all-to-all-start = ((f32[8,1,2048]{2,1,0:T(1,128)}), f32[8,1,2048]{2,1,0:T(1,128)S(1)}, u32[]{:S(2)}, u32[]{:S(2)}) async-start(f32[8,1,2048]{2,1,0:T(1,128)} %reshape.318), calls=%async_computation | async-start | bytes 131072 | tf_op jit(solution)/shard_map/all_to_all | solution.py:77
  168.6 9.2 %all-to-all-start.1 = ((f32[4,1,4096]{2,1,0:T(1,128)}), f32[4,1,4096]{2,1,0:T(1,128)S(1)}, u32[]{:S(2)}, u32[]{:S(2)}) async-start(f32[4,1,4096]{2,1,0:T(1,128)} %reshape.320), calls=%async_computation.1 | async-start | bytes 131072 | tf_op jit(solution)/shard_map/all_to_all | solution.py:92
  177.8 9.0 %all-to-all-start.2 = ((f32[4,1,4096]{2,1,0:T(1,128)}), f32[4,1,4096]{2,1,0:T(1,128)S(1)}, u32[]{:S(2)}, u32[]{:S(2)}) async-start(f32[4,1,4096]{2,1,0:T(1,128)} %reshape.322), calls=%async_computation.2 | async-start | bytes 131072 | tf_op jit(solution)/shard_map/all_to_all | solution.py:93
  190.4 8.3 %all-to-all-start.4 = ((f32[8,1,2048]{2,1,0:T(1,128)}), f32[8,1,2048]{2,1,0:T(1,128)S(1)}, u32[]{:S(2)}, u32[]{:S(2)}) async-start(f32[8,1,2048]{2,1,0:T(1,128)} %reshape.324), calls=%async_computation.4 | async-start | bytes 131072 | tf_op jit(solution)/shard_map/all_to_all | solution.py:109
  198.7 8.3 %all-to-all-start.3 = ((f32[8,1,2048]{2,1,0:T(1,128)}), f32[8,1,2048]{2,1,0:T(1,128)S(1)}, u32[]{:S(2)}, u32[]{:S(2)}) async-start(f32[8,1,2048]{2,1,0:T(1,128)} %reshape.326), calls=%async_computation.3 | async-start | bytes 131072 | tf_op jit(solution)/shard_map/all_to_all | solution.py:108
  218.9 8.3 %all-to-all-start.5 = ((f32[8,1,2048]{2,1,0:T(1,128)}), f32[8,1,2048]{2,1,0:T(1,128)S(1)}, u32[]{:S(2)}, u32[]{:S(2)}) async-start(f32[8,1,2048]{2,1,0:T(1,128)} %reshape.328), calls=%async_computation.5 | async-start | bytes 131072 | tf_op jit(solution)/shard_map/all_to_all | solution.py:148
  227.2 8.3 %all-to-all-start.6 = ((f32[8,1,2048]{2,1,0:T(1,128)}), f32[8,1,2048]{2,1,0:T(1,128)S(1)}, u32[]{:S(2)}, u32[]{:S(2)}) async-start(f32[8,1,2048]{2,1,0:T(1,128)} %reshape.330), calls=%async_computation.6 | async-start | bytes 131072 | tf_op jit(solution)/shard_map/all_to_all | solution.py:149
  239.9 9.0 %all-to-all-start.8 = ((f32[4,1,4096]{2,1,0:T(1,128)}), f32[4,1,4096]{2,1,0:T(1,128)S(1)}, u32[]{:S(2)}, u32[]{:S(2)}) async-start(f32[4,1,4096]{2,1,0:T(1,128)} %reshape.334), calls=%async_computation.8 | async-start | bytes 131072 | tf_op jit(solution)/shard_map/all_to_all | solution.py:165
  248.9 9.0 %all-to-all-start.7 = ((f32[4,1,4096]{2,1,0:T(1,128)}), f32[4,1,4096]{2,1,0:T(1,128)S(1)}, u32[]{:S(2)}, u32[]{:S(2)}) async-start(f32[4,1,4096]{2,1,0:T(1,128)} %reshape.332), calls=%async_computation.7 | async-start | bytes 131072 | tf_op jit(solution)/shard_map/all_to_all | solution.py:164
  260.5 8.3 %all-to-all-start.9 = ((f32[8,1,2048]{2,1,0:T(1,128)}), f32[8,1,2048]{2,1,0:T(1,128)S(1)}, u32[]{:S(2)}, u32[]{:S(2)}) async-start(f32[8,1,2048]{2,1,0:T(1,128)} %reshape.336), calls=%async_computation.9 | async-start | bytes 131072 | tf_op jit(solution)/shard_map/all_to_all | solution.py:170
  291.4 7.7 %copy-start = (f32[44,16,256]{2,1,0:T(8,128)S(1)}, f32[44,16,256]{2,1,0:T(8,128)}, u32[]{:S(2)}) copy-start(f32[44,16,256]{2,1,0:T(8,128)} %get-tuple-element.181) | copy-start | bytes 2162692
  299.1 36.7 %copy-start.1 = (f32[704,256]{1,0:T(8,128)S(1)}, f32[704,256]{1,0:T(8,128)}, u32[]{:S(2)}) copy-start(f32[704,256]{1,0:T(8,128)} %param.10) | copy-start | bytes 2162692
Sparse Core Ops, SparseCore 0:
  77.2 39.2 all-reduce.1
where the time goes:
time: 352 us; the launch traced here: 346 us
  other arithmetic  96.9 us (28%)
  waiting for transfers between devices  77 us (22%)
  local copies, waits for them, and re-layouts  58.1 us (17%)
  matrix products  41.2 us (12%)
  starting transfers between devices  34.2 us (10%)
  blocking collectives  21.4 us (6%)
  between operations  14.6 us (4%)
    psum x1, waiting for transfers between devices, on_device(): totals = lax.psum(partial_value, 'dom')  38.2 us
    scatter-add x1, other arithmetic, on_device(): jnp.zeros((R1, own_rows, BINS), jnp.float32).at[first_row, local_row]  36 us
    sub x88, local copies, waits for them, and re-layouts, kernel_table(): offset = places[:, None, :] - centers[None, :, None]  32 us
    dynamic_update_slice x44, other arithmetic, on_device(): lax.map(partial_profile, place_blocks).reshape(BUNCH_GRP, BINS)  26.7 us
    dot_general x44, matrix products, kick_block(): jnp.einsum('bjp,bj->bp', table_block, volt_block, precision=highest)  24.1 us
    all_gather x1, blocking collectives, on_device(): volt_group = lax.all_gather(volt_slab, 'dom', axis=1, tiled=True)  21.4 us
    dot_general x18, matrix products, contract(): return jnp.einsum(pattern, operand, matrix, precision=highest)  16.3 us
    unnamed x31, local copies, waits for them, and re-layouts  12.5 us
  transfers between devices with their start and end apart: 11, of which 11 were waited for; matrix products, arithmetic and copies ran while one was open for 4% of the time, Pallas kernels for 0%

commit v1 on v0

v1 whole, which is shorter than its diff:
```python
import functools
import math

import jax
import jax.numpy as jnp
import numpy as np
from jax import lax
from jax.experimental import pallas as pl
from jax.experimental.pallas import tpu as pltpu
from jax.sharding import PartitionSpec as P

BINS = 32
LANES = 128
HIST = 2
MESH = pl.DeviceIdType.MESH
SCALE = math.sqrt(0.5 * math.log2(math.e))
HIGHEST = lax.Precision.HIGHEST
VMEM = pl.BlockSpec(memory_space=pltpu.VMEM)


class Sizes:
    def __init__(self, groups, domains, positions, impedance):
        self.G, self.D = groups, domains
        self.bunches, self.parts = positions.shape
        _, _, self.k1, self.k2, self.n3 = impedance.shape
        self.n1, self.n2 = self.k1 * domains, self.k2 * groups
        self.r1 = self.n1 // groups
        self.cycle = self.n1 * self.n2 * self.n3
        self.naq = self.n3 // domains
        self.mlo = LANES // self.naq
        self.mp = self.n2 // self.mlo
        self.rows = self.mp * self.r1
        self.per_row = self.n3 // BINS
        self.blocks = -(-self.bunches // LANES)
        self.wide = self.blocks * LANES


def tables(z):
    lane = np.arange(LANES)
    na = (np.arange(z.D)[:, None] * z.naq + (lane % z.naq)[None, :]).reshape(-1)
    ml = np.tile(lane // z.naq, z.D)
    key = (na // BINS * z.mlo + ml).astype(np.int32)
    fold = (np.arange(BINS)[:, None] == (na % BINS)[None, :]).astype(np.float32)
    k1 = np.arange(z.n1)
    ang = 2 * np.pi * (k1[:, None] * k1[None, :] % z.n1) / z.n1
    first = np.concatenate([np.cos(ang), -np.sin(ang)], 0)
    m = np.arange(z.mp)[:, None] * z.mlo + (lane // z.naq)[None, :]
    plane = z.n1 * z.n2
    ang = -2 * np.pi * (m[:, None, :] * k1[None, :, None] % plane) / plane
    turn = np.stack([np.cos(ang), np.sin(ang)])
    k2 = np.arange(z.n2)
    ang = -2 * np.pi * (m[None] * k2[:, None, None] % z.n2) / z.n2
    second = np.stack([np.cos(ang), np.sin(ang)])
    k3 = np.arange(z.n3)
    ang = 2 * np.pi * (na[:, None] * k3[None, :] % z.n3) / z.n3
    cos, sin = np.cos(ang), np.sin(ang)
    part = np.tile(lane // z.naq, z.D)[:, None]
    third = np.where(
        part == 0,
        np.concatenate([cos, -sin], 1),
        np.where(part == 1, np.concatenate([sin, cos], 1), 0.0),
    )
    back = np.where(
        part % 2 == 0, np.concatenate([cos, -sin], 1), np.concatenate([sin, cos], 1)
    ).T
    f32 = lambda a: np.asarray(a, np.float32)
    return dict(
        key=key[:, None],
        fold=f32(fold),
        spread=f32(fold.T / (z.parts * z.D)),
        first=f32(first),
        first_t=f32(first.T),
        turn=f32(turn),
        second=f32(second),
        third=f32(third / math.sqrt(z.bunches * z.G)),
        back=f32(back / math.sqrt(z.cycle)),
    )


def split(a):
    hi = a.astype(jnp.bfloat16)
    return hi, (a - hi.astype(jnp.float32)).astype(jnp.bfloat16)


def dot(a, b, dims=((1,), (0,))):
    return lax.dot_general(a, b, (dims, ((), ())), preferred_element_type=jnp.float32)


def dot3(a, b):
    ah, al = split(a)
    bh, bl = split(b)
    return dot(ah, bh) + (dot(ah, bl) + dot(al, bh))


def places(z, bucket):
    nb = bucket // z.per_row
    m = nb % z.n2
    row = m // z.mlo * z.r1 + nb // z.n2
    key = bucket % z.per_row * z.mlo + m % z.mlo
    return row, key


def turned(z, ref, blk):
    n = min(LANES, z.bunches - blk * LANES)
    x = ref[blk * LANES : blk * LANES + n, :]
    if n < LANES:
        x = jnp.concatenate([x, jnp.zeros((LANES - n, x.shape[1]), x.dtype)], 0)
    return x.T


def profile_kernel(z, pos, row, key, lane_key, spread, out, prof):
    for blk in range(z.blocks):
        xs = turned(z, pos, blk) * SCALE
        xs = xs.reshape(z.parts // 8, 8, LANES)
        for j in range(BINS):
            t = xs - (j + 0.5) * SCALE
            s = jnp.sum(jnp.exp2(-(t * t)), axis=0)
            prof[j : j + 1, blk * LANES : (blk + 1) * LANES] = jnp.sum(s, axis=0, keepdims=True)
    ids = lax.broadcasted_iota(jnp.int32, (z.rows, z.wide), 0)
    onehot = (ids == row[...]).astype(jnp.float32).astype(jnp.bfloat16)
    ph, plo = split(prof[...])
    sp = spread[...].astype(jnp.bfloat16)
    for d in range(z.D):
        part = slice(d * LANES, (d + 1) * LANES)
        mine = lane_key[part, :] == key[...]
        high = jnp.where(mine, dot(sp[part], ph), 0.0).astype(jnp.bfloat16)
        low = jnp.where(mine, dot(sp[part], plo), 0.0).astype(jnp.bfloat16)
        line = dot(onehot, high, ((1,), (1,))) + dot(onehot, low, ((1,), (1,)))
        out[d] = line.reshape(z.mp, z.r1, LANES)


def greet(z, over):
    barrier = pltpu.get_barrier_semaphore()
    count = 0
    for axis, n in over:
        me = lax.axis_index(axis)
        for k in range(1, n):
            pl.semaphore_signal(
                barrier, inc=1, device_id={axis: lax.rem(me + k, n)}, device_id_type=MESH
            )
        count += n - 1
    pl.semaphore_wait(barrier, count)


def push(axis, n, src_of, dst_of, send, recv):
    me = lax.axis_index(axis)
    copies = []
    for k in range(1, n):
        to = lax.rem(me + k, n)
        c = pltpu.make_async_remote_copy(
            src_ref=src_of(to),
            dst_ref=dst_of(me, k),
            send_sem=send.at[k - 1],
            recv_sem=recv.at[k - 1],
            device_id={axis: to},
            device_id_type=MESH,
        )
        c.start()
        copies.append(c)
    return copies


def forward_comm(z, parts, out, slots, total, s0, r0, s1, r1):
    greet(z, (("dom", z.D), ("grp", z.G)))
    copies = push("dom", z.D, lambda to: parts.at[to], lambda me, k: slots.at[k - 1], s0, r0)
    acc = parts[lax.axis_index("dom")]
    for k, c in enumerate(copies):
        c.wait_recv()
        acc = acc + slots[k]
    total[...] = acc
    g = lax.axis_index("grp")
    rows = lambda i: pl.ds(pl.multiple_of(i * z.r1, z.r1), z.r1)
    more = push("grp", z.G, lambda to: total, lambda me, k: out.at[:, rows(me), :], s1, r1)
    out[:, rows(g), :] = acc
    for c in copies:
        c.wait_send()
    for c in more:
        c.wait()


def swap_comm(z, parts, out, send, recv):
    greet(z, (("dom", z.D),))
    d = lax.axis_index("dom")
    copies = push("dom", z.D, lambda to: parts.at[to], lambda me, k: out.at[me], send, recv)
    out[d] = parts[d]
    for c in copies:
        c.wait()


def backward_comm(z, volt, out, slots, s0, r0, s1, r1):
    greet(z, (("dom", z.D), ("grp", z.G)))
    rows = lambda i: pl.ds(pl.multiple_of(i * z.r1, z.r1), z.r1)
    copies = push(
        "grp", z.G, lambda to: volt.at[:, rows(to), :], lambda me, k: slots.at[k - 1], s0, r0
    )
    acc = volt[:, rows(lax.axis_index("grp")), :]
    for k, c in enumerate(copies):
        c.wait_recv()
        acc = acc + slots[k]
    d = lax.axis_index("dom")
    out[d] = acc
    more = push("dom", z.D, lambda to: out.at[d], lambda me, k: out.at[me], s1, r1)
    for c in copies:
        c.wait_send()
    for c in more:
        c.wait()


def even_lane(z, shape):
    return lax.broadcasted_iota(jnp.int32, shape, len(shape) - 1) // z.naq % 2 == 0


def forward_kernel(z, x, first, turn, second, out, re, im):
    g = lax.axis_index("grp")
    table = first[...]
    for m in range(z.mp):
        a = dot3(table, x[m])
        ar, ai = a[: z.n1], a[z.n1 :]
        re[m] = ar * turn[0, m] - ai * turn[1, m]
        im[m] = ar * turn[1, m] + ai * turn[0, m]
    even = even_lane(z, (z.n1, LANES))
    for k in range(z.k2):
        k2 = g * z.k2 + k
        yr = yi = 0.0
        for m in range(z.mp):
            cr, ci = second[0, k2, m : m + 1, :], second[1, k2, m : m + 1, :]
            yr = yr + (re[m] * cr - im[m] * ci)
            yi = yi + (re[m] * ci + im[m] * cr)
        s = z.naq
        while s < LANES:
            yr = yr + pltpu.roll(yr, s, 1)
            yi = yi + pltpu.roll(yi, s, 1)
            s *= 2
        out[:, k] = jnp.where(even, yr, yi).reshape(z.D, z.k1, LANES)


def middle_kernel(z, y, imp, hist, third, back, spec, out, volt, cs, sn):
    g, d_own = lax.axis_index("grp"), lax.axis_index("dom")
    n = z.k1 * z.k2
    ids = lax.broadcasted_iota(jnp.int32, (n, LANES), 0)
    lane = lax.broadcasted_iota(jnp.int32, (n, LANES), 1)
    freq = d_own * z.k1 + ids % z.k1 + z.n1 * (g * z.k2 + ids // z.k1)
    even = even_lane(z, (n, LANES))
    total = jnp.zeros((n, 2 * z.n3), jnp.float32)
    for d in range(z.D):
        ang = (freq * (lane % z.naq + d * z.naq) % z.cycle).astype(jnp.float32)
        ang = ang * (2 * math.pi / z.cycle)
        c, s = jnp.cos(ang), jnp.sin(ang)
        s = jnp.where(even, s, -s)
        cs[d], sn[d] = c, s
        p = y[d].reshape(n, LANES)
        p = p * c + pltpu.roll(p, z.naq, 1) * s
        total = total + dot3(p, third[d * LANES : (d + 1) * LANES, :])
    for k in range(z.k2):
        rows = slice(k * z.k1, (k + 1) * z.k1)
        sr, si = total[rows, : z.n3], total[rows, z.n3 :]
        spec[0, :, k, :] = sr
        spec[1, :, k, :] = si
        vr = imp[0, 0, :, k, :] * sr - imp[0, 1, :, k, :] * si
        vi = imp[0, 0, :, k, :] * si + imp[0, 1, :, k, :] * sr
        for h in range(HIST):
            ir, ii = imp[h + 1, 0, :, k, :], imp[h + 1, 1, :, k, :]
            hr, hi = hist[h, 0, :, k, :], hist[h, 1, :, k, :]
            vr = vr + ir * hr - ii * hi
            vi = vi + ir * hi + ii * hr
        volt[rows, : z.n3] = vr
        volt[rows, z.n3 :] = vi
    v = volt[...]
    for d in range(z.D):
        p = dot3(v, back[:, d * LANES : (d + 1) * LANES])
        p = p * cs[d] - pltpu.roll(p, z.naq, 1) * sn[d]
        out[d] = p.reshape(z.k2, z.k1, LANES)


def backward_kernel(z, q, first_t, turn, second, out, re, im):
    g = lax.axis_index("grp")
    even = even_lane(z, (z.n1, LANES))
    for k in range(z.k2):
        p = q[:, k].reshape(z.n1, LANES)
        r = pltpu.roll(p, z.naq, 1)
        re[k] = jnp.where(even, p, r)
        im[k] = jnp.where(even, r, p)
    table = first_t[...]
    for m in range(z.mp):
        ur = ui = 0.0
        for k in range(z.k2):
            k2 = g * z.k2 + k
            cr, ci = second[0, k2, m : m + 1, :], second[1, k2, m : m + 1, :]
            ur = ur + (re[k] * cr + im[k] * ci)
            ui = ui + (im[k] * cr - re[k] * ci)
        tr, ti = turn[0, m], turn[1, m]
        u = jnp.concatenate([ur * tr + ui * ti, ui * tr - ur * ti], 0)
        out[m] = dot3(table, u)


def kick_kernel(z, pos, ener, row, key, lane_key, fold, w, pos_out, ener_out, volts, xt, kt):
    ids = lax.broadcasted_iota(jnp.int32, (z.rows, z.wide), 0)
    onehot = (ids == row[...]).astype(jnp.float32).astype(jnp.bfloat16)
    rows_t = jnp.zeros((BINS, z.wide), jnp.float32)
    fo = fold[...].astype(jnp.bfloat16)
    for d in range(z.D):
        part = slice(d * LANES, (d + 1) * LANES)
        mine = lane_key[part, :] == key[...]
        wh, wl = split(w[d].reshape(z.rows, LANES).T)
        high = jnp.where(mine, dot(wh, onehot), 0.0).astype(jnp.bfloat16)
        low = jnp.where(mine, dot(wl, onehot), 0.0).astype(jnp.bfloat16)
        rows_t = rows_t + (dot(fo[:, part], high) + dot(fo[:, part], low))
    volts[...] = rows_t
    step = 64
    for blk in range(z.blocks):
        n = min(LANES, z.bunches - blk * LANES)
        xt[...] = turned(z, pos, blk) * SCALE

        def some(i, carry):
            at = pl.ds(pl.multiple_of(i * step, step), step)
            xs = xt[at, :]
            num = jnp.zeros((step, LANES), jnp.float32)
            den = jnp.zeros((step, LANES), jnp.float32)
            for j in range(BINS):
                t = xs - (j + 0.5) * SCALE
                e = jnp.exp2(-(t * t))
                num = num + e * volts[j : j + 1, blk * LANES : (blk + 1) * LANES]
                den = den + e
            kt[at, :] = num / den
            return carry

        lax.fori_loop(0, z.parts // step, some, 0)
        rows = slice(blk * LANES, blk * LANES + n)
        x = pos[rows, :]
        turn = jnp.sin((2 * math.pi / BINS) * (x - 0.5 * BINS))
        e = ener[rows, :] - 0.5 * turn - kt[...].T[:n]
        ener_out[rows, :] = e
        pos_out[rows, :] = x + 0.25 * e


def call(body, z, outs, args, scratch=(), collective=None):
    params = dict(vmem_limit_bytes=48 * 2**20)
    if collective is not None:
        params.update(collective_id=collective, has_side_effects=True)
    shapes = [jax.ShapeDtypeStruct(s, jnp.float32) for s in outs]
    return pl.pallas_call(
        functools.partial(body, z),
        out_shape=shapes if len(shapes) > 1 else shapes[0],
        in_specs=[VMEM] * len(args),
        out_specs=[VMEM] * len(shapes) if len(shapes) > 1 else VMEM,
        scratch_shapes=list(scratch),
        compiler_params=pltpu.CompilerParams(**params),
    )(*args)


def on_device(positions, energies, bucket, impedance, history):
    z = Sizes(lax.axis_size("grp"), lax.axis_size("dom"), positions, impedance)
    t = tables(z)
    f32 = lambda *s: pltpu.VMEM(s, jnp.float32)
    dma = lambda n: pltpu.SemaphoreType.DMA((n,))
    row, key = places(z, bucket)
    pad = ((0, 0), (0, z.wide - z.bunches))
    row = jnp.pad(row[None, :], pad, constant_values=-1)
    key = jnp.pad(key[None, :], pad, constant_values=-1)
    slab = (z.mp, z.r1, LANES)
    full = (z.mp, z.n1, LANES)
    chunk = (z.D, z.k2, z.k1, LANES)
    parts = call(
        profile_kernel, z, [(z.D,) + slab],
        (positions, row, key, t["key"], t["spread"]), [f32(BINS, z.wide)],
    )
    x = call(
        forward_comm, z, [full], (parts,),
        [f32(z.D - 1, *slab), f32(*slab), dma(z.D - 1), dma(z.D - 1), dma(z.G - 1), dma(z.G - 1)],
        0,
    )
    y = call(
        forward_kernel, z, [chunk], (x, t["first"], t["turn"], t["second"]),
        [f32(*full), f32(*full)],
    )
    y = call(swap_comm, z, [chunk], (y,), [dma(z.D - 1), dma(z.D - 1)], 1)
    n = z.k1 * z.k2
    spectrum, q = call(
        middle_kernel, z, [(2, z.k1, z.k2, z.n3), chunk],
        (y, impedance, history, t["third"], t["back"]),
        [f32(n, 2 * z.n3), f32(z.D, n, LANES), f32(z.D, n, LANES)],
    )
    q = call(swap_comm, z, [chunk], (q,), [dma(z.D - 1), dma(z.D - 1)], 1)
    volt = call(
        backward_kernel, z, [full], (q, t["first_t"], t["turn"], t["second"]),
        [f32(z.k2, z.n1, LANES), f32(z.k2, z.n1, LANES)],
    )
    w = call(
        backward_comm, z, [(z.D,) + slab], (volt,),
        [f32(z.G - 1, *slab), dma(z.G - 1), dma(z.G - 1), dma(z.D - 1), dma(z.D - 1)],
        2,
    )
    pos_out, ener_out = call(
        kick_kernel, z, [positions.shape, positions.shape],
        (positions, energies, row, key, t["key"], t["fold"], w),
        [f32(BINS, z.wide), f32(z.parts, LANES), f32(z.parts, LANES)],
    )
    return pos_out, ener_out, spectrum


def solution(mesh):
    placed = (
        P("grp", "dom"),
        P("grp", "dom"),
        P("grp"),
        P(None, None, "dom", "grp", None),
        P(None, None, "dom", "grp", None),
    )
    return jax.shard_map(
        on_device,
        mesh=mesh,
        in_specs=placed,
        out_specs=(P("grp", "dom"), P("grp", "dom"), P(None, "dom", "grp", None)),
        check_vma=False,
    )
```

time: 352 us -> 73.9 us (0.21); the launches traced: 346 us -> 73.6 us
  other arithmetic: 96.9 us -> 0.71 us
  waiting for transfers between devices: 77 us -> 0 us
  Pallas kernels: 0 us -> 68.9 us
  local copies, waits for them, and re-layouts: 58.1 us -> 3.1 us
  matrix products: 41.2 us -> 0 us
  starting transfers between devices: 34.2 us -> 0 us
  blocking collectives: 21.4 us -> 0 us
  between operations: 14.6 us -> 0.88 us
    pallas_call x0 -> x9, Pallas kernels: none -> 68.9 us  [call(): pl.pallas_call(functools.partial(body, z), out_shape=shapes if len(shapes...]
    dot_general x62 -> x0, matrix products: 40.4 us -> none  [the longest x44 24.1 us: kick_block(): jnp.einsum('bjp,bj->bp', table_block, volt_block, precision=highest)]
    all_to_all x10 -> x0, waiting for transfers between devices: 38.8 us -> none  [the longest x1 4.95 us: on_device(): lax.all_to_all(density, 'grp', split_axis=2, concat_axis=0, tiled=True)]
    psum x1 -> x0, waiting for transfers between devices: 38.2 us -> none  [on_device(): totals = lax.psum(partial_value, 'dom')]
    scatter-add x1 -> x0, other arithmetic: 36 us -> none  [on_device(): jnp.zeros((R1, own_rows, BINS), jnp.float32).at[first_row, local_row]]
    all_to_all x10 -> x0, starting transfers between devices: 34.1 us -> none  [the longest x1 3.66 us: on_device(): lax.all_to_all(density, 'grp', split_axis=2, concat_axis=0, tiled=True)]
    sub x92 -> x0, local copies, waits for them, and re-layouts: 32.7 us -> none  [the longest x88 32 us: kernel_table(): offset = places[:, None, :] - centers[None, :, None]]
    dynamic_update_slice x88 -> x0, other arithmetic: 27.2 us -> none  [the longest x44 26.7 us: on_device(): lax.map(partial_profile, place_blocks).reshape(BUNCH_GRP, BINS)]
  transfers between devices with their start and end apart: 11 -> 0, of which waited for: 11 -> 0; matrix products, arithmetic and copies ran while one was open for 4% -> 0% of each run, Pallas kernels for 0% -> 0%
where the time goes in v1:
time: 73.9 us; the launch traced here: 73.6 us
  Pallas kernels  68.9 us (93%)
  local copies, waits for them, and re-layouts  3.1 us (4%)
  between operations  0.88 us (1%)
    pallas_call x9, Pallas kernels, call(): pl.pallas_call(functools.partial(body, z), out_shape=shapes if len(shapes...  68.9 us
    unnamed x30, local copies, waits for them, and re-layouts  3.08 us

profile of v1, /device:TPU:0, one launch (start us, length us, event | category | flops | bytes accessed | tf_op | source)
XLA Modules:
  0.0 73.6 jit_solution(769767851058959973)
XLA Ops:
  0.6 0.7 fusion.3
  1.4 0.0 copy-start.1
  1.4 1.1 %copy-done.1 = f32[704,256]{1,0:T(8,128)S(1)} copy-done((f32[704,256]{1,0:T(8,128)S(1)}, f32[704,256]{1,0:T(8,128)}, u32[]{:S(2)}) %copy-start.1) | copy-done | bytes 720920
  2.5 0.9 %copy-done.4 = s32[512,1]{1,0:T(8,128)S(1)} copy-done((s32[512,1]{1,0:T(8,128)S(1)}, s32[512,1]{1,0:T(8,128)}, u32[]{:S(2)}) %copy-start.4) | copy-done | bytes 2072
  3.5 0.9 %copy-done.10 = f32[512,32]{1,0:T(8,128)S(1)} copy-done((f32[512,32]{1,0:T(8,128)S(1)}, f32[512,32]{1,0:T(8,128)}, u32[]{:S(2)}) %copy-start.10) | copy-done | bytes 65560
  4.4 6.3 %shard_map.157.parts = f32[4,16,8,128]{3,2,1,0:T(8,128)S(1)} custom-call(f32[704,256]{1,0:T(8,128)S(1)} %copy-done.1, s32[1,768]{1,0:T(1,128)S(1)} %pad.7.row, s32[1,768]{1,0:T(1,128)S(1)} %pad.8.key, s32[512,1]{1,0:T(8,128)S(1)} %copy-done.4, f32[512,32]{1,0:T(8,128)S(1)} %copy-done.10), custom_call_target="tpu_custom_call" | custom-call | tf_op jit(solution)/shard_map/pallas_call | solution.py:341
  10.8 0.0 copy-start.3
  10.8 0.0 copy-start.11
  10.8 16.7 %shard_map.158.x = f32[16,64,128]{2,1,0:T(8,128)S(1)} custom-call(f32[4,16,8,128]{3,2,1,0:T(8,128)S(1)} %shard_map.157.parts), custom_call_target="tpu_custom_call" | custom-call | tf_op jit(solution)/shard_map/pallas_call | solution.py:341
  27.5 0.0 copy-done
  27.5 0.0 copy-done.13
  27.6 0.0 copy-done.3
  27.6 0.0 copy-start.6
  27.6 0.0 copy-start.7
  27.6 0.0 copy-start.9
  27.6 1.0 %shard_map.159.parts = f32[4,4,16,128]{3,2,1,0:T(8,128)S(1)} custom-call(f32[16,64,128]{2,1,0:T(8,128)S(1)} %shard_map.158.x, f32[128,64]{1,0:T(8,128)S(1)} %copy-done.13, f32[2,16,64,128]{3,2,1,0:T(8,128)S(1)} %copy-done, f32[2,32,16,128]{3,2,1,0:T(8,128)S(1)} %copy-done.3), custom_call_target="tpu_custom_call" | custom-call | tf_op jit(solution)/shard_map/pallas_call | solution.py:341
  28.6 8.0 %shard_map.160.y = f32[4,4,16,128]{3,2,1,0:T(8,128)S(1)} custom-call(f32[4,4,16,128]{3,2,1,0:T(8,128)S(1)} %shard_map.159.parts), custom_call_target="tpu_custom_call" | custom-call | tf_op jit(solution)/shard_map/pallas_call | solution.py:341
  36.6 0.0 copy-done.11
  36.7 0.0 copy-done.6
  36.7 1.8 %shard_map.161 = (f32[2,16,4,256]{3,2,1,0:T(4,128)}, f32[4,4,16,128]{3,2,1,0:T(8,128)S(1)}) custom-call(f32[4,4,16,128]{3,2,1,0:T(8,128)S(1)} %shard_map.160.y, f32[3,2,16,4,256]{4,3,2,1,0:T(4,128)S(1)} %copy-done.9, f32[2,2,16,4,256]{4,3,2,1,0:T(4,128)S(1)} %copy-done.11, f32[512,512]{1,0:T(8,128)S(1)} %copy-done.7, f32[512,512]{1,0:T(8,128)S(1)} %copy-done.6), custom_call_target="tpu_custom_call" | custom-call | tf_op jit(solution)/shard_map/pallas_call | solution.py:341
  38.4 5.8 %shard_map.162.q = f32[4,4,16,128]{3,2,1,0:T(8,128)S(1)} custom-call(f32[4,4,16,128]{3,2,1,0:T(8,128)S(1)} %get-tuple-element.7.parts), custom_call_target="tpu_custom_call" | custom-call | tf_op jit(solution)/shard_map/pallas_call | solution.py:341
  44.2 0.0 copy-start.5
  44.2 0.0 copy-start.8
  44.3 1.0 %shard_map.163.volt = f32[16,64,128]{2,1,0:T(8,128)S(1)} custom-call(f32[4,4,16,128]{3,2,1,0:T(8,128)S(1)} %shard_map.162.q, f32[64,128]{1,0:T(8,128)S(1)} %copy-done.14, f32[2,16,64,128]{3,2,1,0:T(8,128)S(1)} %copy-done, f32[2,32,16,128]{3,2,1,0:T(8,128)S(1)} %copy-done.3), custom_call_target="tpu_custom_call" | custom-call | tf_op jit(solution)/shard_map/pallas_call | solution.py:341
  45.3 0.0 copy-start.2
  45.3 0.0 copy-start.12
  45.3 17.0 %shard_map.164.w = f32[4,16,8,128]{3,2,1,0:T(8,128)S(1)} custom-call(f32[16,64,128]{2,1,0:T(8,128)S(1)} %shard_map.163.volt), custom_call_target="tpu_custom_call" | custom-call | tf_op jit(solution)/shard_map/pallas_call | solution.py:341
  62.4 0.0 copy-done.5
  62.4 0.0 copy-done.8
  62.4 0.0 copy-done.2
  62.4 0.0 copy-done.12
  62.4 11.2 %shard_map.165 = (f32[704,256]{1,0:T(8,128)}, f32[704,256]{1,0:T(8,128)}) custom-call(f32[704,256]{1,0:T(8,128)S(1)} %copy-done.2, f32[704,256]{1,0:T(8,128)S(1)} %copy-done.8, s32[1,768]{1,0:T(1,128)S(1)} %pad.7.row, s32[1,768]{1,0:T(1,128)S(1)} %pad.8.key, s32[512,1]{1,0:T(8,128)S(1)} %copy-done.5, f32[32,512]{1,0:T(8,128)S(1)} %copy-done.12, ...), custom_call_target="tpu_custom_call" | custom-call | tf_op jit(solution)/shard_map/pallas_call | solution.py:341
  (12 shorter events, 0.0 us)
Async XLA Ops:
  1.4 1.1 %copy-start.1 = (f32[704,256]{1,0:T(8,128)S(1)}, f32[704,256]{1,0:T(8,128)}, u32[]{:S(2)}) copy-start(f32[704,256]{1,0:T(8,128)} %pos.3) | copy-start | bytes 2162692
  2.5 0.9 %copy-start.4 = (s32[512,1]{1,0:T(8,128)S(1)}, s32[512,1]{1,0:T(8,128)}, u32[]{:S(2)}) copy-start(s32[512,1]{1,0:T(8,128)} %constant.87.clone.lane_key) | copy-start | bytes 6148
  3.5 0.9 %copy-start.10 = (f32[512,32]{1,0:T(8,128)S(1)}, f32[512,32]{1,0:T(8,128)}, u32[]{:S(2)}) copy-start(f32[512,32]{1,0:T(8,128)} %constant.88.clone.spread) | copy-start | bytes 196612
  4.4 23.1 %copy-start = (f32[2,16,64,128]{3,2,1,0:T(8,128)S(1)}, f32[2,16,64,128]{3,2,1,0:T(8,128)}, u32[]{:S(2)}) copy-start(f32[2,16,64,128]{3,2,1,0:T(8,128)} %constant.90.clone.turn) | copy-start | bytes 3145732
  4.4 23.1 %copy-start.13 = (f32[128,64]{1,0:T(8,128)S(1)}, f32[128,64]{1,0:T(8,128)}, u32[]{:S(2)}) copy-start(f32[128,64]{1,0:T(8,128)} %constant.89.clone.first) | copy-start | bytes 98308
  10.8 16.8 %copy-start.3 = (f32[2,32,16,128]{3,2,1,0:T(8,128)S(1)}, f32[2,32,16,128]{3,2,1,0:T(8,128)}, u32[]{:S(2)}) copy-start(f32[2,32,16,128]{3,2,1,0:T(8,128)} %constant.91.clone.second) | copy-start | bytes 1572868
  10.8 25.9 %copy-start.11 = (f32[2,2,16,4,256]{4,3,2,1,0:T(4,128)S(1)}, f32[2,2,16,4,256]{4,3,2,1,0:T(4,128)}, u32[]{:S(2)}) copy-start(f32[2,2,16,4,256]{4,3,2,1,0:T(4,128)} %hist.1) | copy-start | bytes 786436
  27.6 9.1 %copy-start.6 = (f32[512,512]{1,0:T(8,128)S(1)}, f32[512,512]{1,0:T(8,128)}, u32[]{:S(2)}) copy-start(f32[512,512]{1,0:T(8,128)} %constant.93.clone.back) | copy-start | bytes 3145732
  27.6 9.1 %copy-start.7 = (f32[512,512]{1,0:T(8,128)S(1)}, f32[512,512]{1,0:T(8,128)}, u32[]{:S(2)}) copy-start(f32[512,512]{1,0:T(8,128)} %constant.92.clone.third) | copy-start | bytes 3145732
  27.6 9.1 %copy-start.9 = (f32[3,2,16,4,256]{4,3,2,1,0:T(4,128)S(1)}, f32[3,2,16,4,256]{4,3,2,1,0:T(4,128)}, u32[]{:S(2)}) copy-start(f32[3,2,16,4,256]{4,3,2,1,0:T(4,128)} %imp.1) | copy-start | bytes 1179652
  38.4 5.8 %copy-start.14 = (f32[64,128]{1,0:T(8,128)S(1)}, f32[64,128]{1,0:T(8,128)}, u32[]{:S(2)}) copy-start(f32[64,128]{1,0:T(8,128)} %constant.94.clone.first_t) | copy-start | bytes 98308
  44.2 18.1 %copy-start.5 = (s32[512,1]{1,0:T(8,128)S(1)}, s32[512,1]{1,0:T(8,128)}, u32[]{:S(2)}) copy-start(s32[512,1]{1,0:T(8,128)} %constant.87.clone.lane_key) | copy-start | bytes 6148
  44.2 18.1 %copy-start.8 = (f32[704,256]{1,0:T(8,128)S(1)}, f32[704,256]{1,0:T(8,128)}, u32[]{:S(2)}) copy-start(f32[704,256]{1,0:T(8,128)} %ener.1) | copy-start | bytes 2162692
  45.3 17.1 %copy-start.2 = (f32[704,256]{1,0:T(8,128)S(1)}, f32[704,256]{1,0:T(8,128)}, u32[]{:S(2)}) copy-start(f32[704,256]{1,0:T(8,128)} %pos.3) | copy-start | bytes 2162692
  45.3 17.1 %copy-start.12 = (f32[32,512]{1,0:T(8,128)S(1)}, f32[32,512]{1,0:T(8,128)}, u32[]{:S(2)}) copy-start(f32[32,512]{1,0:T(8,128)} %constant.95.clone.fold) | copy-start | bytes 196612

commit v2 on v1

--- a/solution.py
+++ b/solution.py
@@ -27,6 +27,7 @@
         self.r1 = self.n1 // groups
         self.cycle = self.n1 * self.n2 * self.n3
         self.naq = self.n3 // domains
+        self.jb = BINS // domains
         self.mlo = LANES // self.naq
         self.mp = self.n2 // self.mlo
         self.rows = self.mp * self.r1
@@ -37,10 +38,10 @@
 
 def tables(z):
     lane = np.arange(LANES)
-    na = (np.arange(z.D)[:, None] * z.naq + (lane % z.naq)[None, :]).reshape(-1)
-    ml = np.tile(lane // z.naq, z.D)
-    key = (na // BINS * z.mlo + ml).astype(np.int32)
-    fold = (np.arange(BINS)[:, None] == (na % BINS)[None, :]).astype(np.float32)
+    q = lane % z.naq
+    na = q // z.jb * BINS + np.arange(z.D)[:, None] * z.jb + q % z.jb
+    na = na.reshape(-1)
+    key = (q // z.jb * z.mlo + lane // z.naq).astype(np.int32)
     k1 = np.arange(z.n1)
     ang = 2 * np.pi * (k1[:, None] * k1[None, :] % z.n1) / z.n1
     first = np.concatenate([np.cos(ang), -np.sin(ang)], 0)
@@ -66,8 +67,6 @@
     f32 = lambda a: np.asarray(a, np.float32)
     return dict(
         key=key[:, None],
-        fold=f32(fold),
-        spread=f32(fold.T / (z.parts * z.D)),
         first=f32(first),
         first_t=f32(first.T),
         turn=f32(turn),
@@ -108,25 +107,43 @@
     return x.T
 
 
-def profile_kernel(z, pos, row, key, lane_key, spread, out, prof):
+def profile_kernel(z, pos, out):
     for blk in range(z.blocks):
         xs = turned(z, pos, blk) * SCALE
         xs = xs.reshape(z.parts // 8, 8, LANES)
+        cols = slice(blk * LANES, (blk + 1) * LANES)
         for j in range(BINS):
             t = xs - (j + 0.5) * SCALE
             s = jnp.sum(jnp.exp2(-(t * t)), axis=0)
-            prof[j : j + 1, blk * LANES : (blk + 1) * LANES] = jnp.sum(s, axis=0, keepdims=True)
+            at = slice(j % z.jb, j % z.jb + 1)
+            out[j // z.jb, at, cols] = jnp.sum(s, axis=0, keepdims=True)
+
+
+def found(z, idx, lane_key, g):
     ids = lax.broadcasted_iota(jnp.int32, (z.rows, z.wide), 0)
-    onehot = (ids == row[...]).astype(jnp.float32).astype(jnp.bfloat16)
-    ph, plo = split(prof[...])
-    sp = spread[...].astype(jnp.bfloat16)
-    for d in range(z.D):
-        part = slice(d * LANES, (d + 1) * LANES)
-        mine = lane_key[part, :] == key[...]
-        high = jnp.where(mine, dot(sp[part], ph), 0.0).astype(jnp.bfloat16)
-        low = jnp.where(mine, dot(sp[part], plo), 0.0).astype(jnp.bfloat16)
-        line = dot(onehot, high, ((1,), (1,))) + dot(onehot, low, ((1,), (1,)))
-        out[d] = line.reshape(z.mp, z.r1, LANES)
+    onehot = (ids == idx[g, 0:1, :]).astype(jnp.float32).astype(jnp.bfloat16)
+    return onehot, lane_key[...] == idx[g, 1:2, :]
+
+
+def scatter(z, prof, idx, lane_key, x):
+    for g in range(z.G):
+        onehot, mine = found(z, idx, lane_key, g)
+        p = prof[g] * (1.0 / (z.parts * z.D))
+        ph = p.astype(jnp.bfloat16).astype(jnp.float32)
+        spread = lambda a: jnp.where(mine, jnp.concatenate([a] * (LANES // z.jb), 0), 0.0)
+        both = jnp.concatenate([spread(ph), spread(p - ph)], 0).astype(jnp.bfloat16)
+        line = dot(onehot, both, ((1,), (1,)))
+        line = line[:, :LANES] + line[:, LANES:]
+        x[:, g * z.r1 : (g + 1) * z.r1, :] = line.reshape(z.mp, z.r1, LANES)
+
+
+def gather(z, volt, idx, lane_key, out):
+    for g in range(z.G):
+        onehot, mine = found(z, idx, lane_key, g)
+        w = volt[:, g * z.r1 : (g + 1) * z.r1, :].reshape(z.rows, LANES).T
+        both = dot(jnp.concatenate(split(w), 0), onehot)
+        both = jnp.where(mine, both[:LANES] + both[LANES:], 0.0)
+        out[g] = jnp.sum(both.reshape(LANES // z.jb, z.jb, z.wide), axis=0)
 
 
 def greet(z, over):
@@ -160,21 +177,22 @@
     return copies
 
 
-def forward_comm(z, parts, out, slots, total, s0, r0, s1, r1):
+def forward_comm(z, parts, idx, out, idx_out, slots, total, s0, r0, s1, r1, s2, r2):
     greet(z, (("dom", z.D), ("grp", z.G)))
     copies = push("dom", z.D, lambda to: parts.at[to], lambda me, k: slots.at[k - 1], s0, r0)
+    copies_i = push("grp", z.G, lambda to: idx, lambda me, k: idx_out.at[me], s2, r2)
+    g = lax.axis_index("grp")
+    idx_out[g] = idx[...]
     acc = parts[lax.axis_index("dom")]
     for k, c in enumerate(copies):
         c.wait_recv()
         acc = acc + slots[k]
     total[...] = acc
-    g = lax.axis_index("grp")
-    rows = lambda i: pl.ds(pl.multiple_of(i * z.r1, z.r1), z.r1)
-    more = push("grp", z.G, lambda to: total, lambda me, k: out.at[:, rows(me), :], s1, r1)
-    out[:, rows(g), :] = acc
+    more = push("grp", z.G, lambda to: total, lambda me, k: out.at[me], s1, r1)
+    out[g] = acc
     for c in copies:
         c.wait_send()
-    for c in more:
+    for c in copies_i + more:
         c.wait()
 
 
@@ -189,11 +207,8 @@
 
 def backward_comm(z, volt, out, slots, s0, r0, s1, r1):
     greet(z, (("dom", z.D), ("grp", z.G)))
-    rows = lambda i: pl.ds(pl.multiple_of(i * z.r1, z.r1), z.r1)
-    copies = push(
-        "grp", z.G, lambda to: volt.at[:, rows(to), :], lambda me, k: slots.at[k - 1], s0, r0
-    )
-    acc = volt[:, rows(lax.axis_index("grp")), :]
+    copies = push("grp", z.G, lambda to: volt.at[to], lambda me, k: slots.at[k - 1], s0, r0)
+    acc = volt[lax.axis_index("grp")]
     for k, c in enumerate(copies):
         c.wait_recv()
         acc = acc + slots[k]
@@ -210,7 +225,8 @@
     return lax.broadcasted_iota(jnp.int32, shape, len(shape) - 1) // z.naq % 2 == 0
 
 
-def forward_kernel(z, x, first, turn, second, out, re, im):
+def forward_kernel(z, prof, idx, lane_key, first, turn, second, out, x, re, im):
+    scatter(z, prof, idx, lane_key, x)
     g = lax.axis_index("grp")
     table = first[...]
     for m in range(z.mp):
@@ -243,7 +259,9 @@
     even = even_lane(z, (n, LANES))
     total = jnp.zeros((n, 2 * z.n3), jnp.float32)
     for d in range(z.D):
-        ang = (freq * (lane % z.naq + d * z.naq) % z.cycle).astype(jnp.float32)
+        q = lane % z.naq
+        na = q // z.jb * BINS + q % z.jb + d * z.jb
+        ang = (freq * na % z.cycle).astype(jnp.float32)
         ang = ang * (2 * math.pi / z.cycle)
         c, s = jnp.cos(ang), jnp.sin(ang)
         s = jnp.where(even, s, -s)
@@ -272,7 +290,7 @@
         out[d] = p.reshape(z.k2, z.k1, LANES)
 
 
-def backward_kernel(z, q, first_t, turn, second, out, re, im):
+def backward_kernel(z, q, idx, lane_key, first_t, turn, second, out, volt, re, im):
     g = lax.axis_index("grp")
     even = even_lane(z, (z.n1, LANES))
     for k in range(z.k2):
@@ -290,22 +308,11 @@
             ui = ui + (im[k] * cr - re[k] * ci)
         tr, ti = turn[0, m], turn[1, m]
         u = jnp.concatenate([ur * tr + ui * ti, ui * tr - ur * ti], 0)
-        out[m] = dot3(table, u)
-
-
-def kick_kernel(z, pos, ener, row, key, lane_key, fold, w, pos_out, ener_out, volts, xt, kt):
-    ids = lax.broadcasted_iota(jnp.int32, (z.rows, z.wide), 0)
-    onehot = (ids == row[...]).astype(jnp.float32).astype(jnp.bfloat16)
-    rows_t = jnp.zeros((BINS, z.wide), jnp.float32)
-    fo = fold[...].astype(jnp.bfloat16)
-    for d in range(z.D):
-        part = slice(d * LANES, (d + 1) * LANES)
-        mine = lane_key[part, :] == key[...]
-        wh, wl = split(w[d].reshape(z.rows, LANES).T)
-        high = jnp.where(mine, dot(wh, onehot), 0.0).astype(jnp.bfloat16)
-        low = jnp.where(mine, dot(wl, onehot), 0.0).astype(jnp.bfloat16)
-        rows_t = rows_t + (dot(fo[:, part], high) + dot(fo[:, part], low))
-    volts[...] = rows_t
+        volt[m] = dot3(table, u)
+    gather(z, volt, idx, lane_key, out)
+
+
+def kick_kernel(z, pos, ener, w, pos_out, ener_out, xt, kt):
     step = 64
     for blk in range(z.blocks):
         n = min(LANES, z.bunches - blk * LANES)
@@ -319,7 +326,8 @@
             for j in range(BINS):
                 t = xs - (j + 0.5) * SCALE
                 e = jnp.exp2(-(t * t))
-                num = num + e * volts[j : j + 1, blk * LANES : (blk + 1) * LANES]
+                at_j = slice(j % z.jb, j % z.jb + 1)
+                num = num + e * w[j // z.jb, at_j, blk * LANES : (blk + 1) * LANES]
                 den = den + e
             kt[at, :] = num / den
             return carry
@@ -337,7 +345,7 @@
     params = dict(vmem_limit_bytes=48 * 2**20)
     if collective is not None:
         params.update(collective_id=collective, has_side_effects=True)
-    shapes = [jax.ShapeDtypeStruct(s, jnp.float32) for s in outs]
+    shapes = [s if hasattr(s, "dtype") else jax.ShapeDtypeStruct(s, jnp.float32) for s in outs]
     return pl.pallas_call(
         functools.partial(body, z),
         out_shape=shapes if len(shapes) > 1 else shapes[0],
@@ -355,23 +363,22 @@
     dma = lambda n: pltpu.SemaphoreType.DMA((n,))
     row, key = places(z, bucket)
     pad = ((0, 0), (0, z.wide - z.bunches))
-    row = jnp.pad(row[None, :], pad, constant_values=-1)
-    key = jnp.pad(key[None, :], pad, constant_values=-1)
-    slab = (z.mp, z.r1, LANES)
+    idx = jnp.pad(jnp.stack([row, key]), pad, constant_values=-1)
+    lane_key = t["key"]
     full = (z.mp, z.n1, LANES)
+    piece = (z.jb, z.wide)
     chunk = (z.D, z.k2, z.k1, LANES)
-    parts = call(
-        profile_kernel, z, [(z.D,) + slab],
-        (positions, row, key, t["key"], t["spread"]), [f32(BINS, z.wide)],
-    )
-    x = call(
-        forward_comm, z, [full], (parts,),
-        [f32(z.D - 1, *slab), f32(*slab), dma(z.D - 1), dma(z.D - 1), dma(z.G - 1), dma(z.G - 1)],
+    parts = call(profile_kernel, z, [(z.D,) + piece], (positions,))
+    prof, idx = call(
+        forward_comm, z,
+        [(z.G,) + piece, jax.ShapeDtypeStruct((z.G,) + idx.shape, jnp.int32)],
+        (parts, idx),
+        [f32(z.D - 1, *piece), f32(*piece), dma(z.D - 1), dma(z.D - 1)] + [dma(z.G - 1)] * 4,
         0,
     )
     y = call(
-        forward_kernel, z, [chunk], (x, t["first"], t["turn"], t["second"]),
-        [f32(*full), f32(*full)],
+        forward_kernel, z, [chunk], (prof, idx, lane_key, t["first"], t["turn"], t["second"]),
+        [f32(*full), f32(*full), f32(*full)],
     )
     y = call(swap_comm, z, [chunk], (y,), [dma(z.D - 1), dma(z.D - 1)], 1)
     n = z.k1 * z.k2
@@ -382,18 +389,18 @@
     )
     q = call(swap_comm, z, [chunk], (q,), [dma(z.D - 1), dma(z.D - 1)], 1)
     volt = call(
-        backward_kernel, z, [full], (q, t["first_t"], t["turn"], t["second"]),
-        [f32(z.k2, z.n1, LANES), f32(z.k2, z.n1, LANES)],
+        backward_kernel, z, [(z.G,) + piece], (q, idx, lane_key, t["first_t"], t["turn"], t["second"]),
+        [f32(*full), f32(z.k2, z.n1, LANES), f32(z.k2, z.n1, LANES)],
     )
     w = call(
-        backward_comm, z, [(z.D,) + slab], (volt,),
-        [f32(z.G - 1, *slab), dma(z.G - 1), dma(z.G - 1), dma(z.D - 1), dma(z.D - 1)],
+        backward_comm, z, [(z.D,) + piece], (volt,),
+        [f32(z.G - 1, *piece), dma(z.G - 1), dma(z.G - 1), dma(z.D - 1), dma(z.D - 1)],
         2,
     )
     pos_out, ener_out = call(
         kick_kernel, z, [positions.shape, positions.shape],
-        (positions, energies, row, key, t["key"], t["fold"], w),
-        [f32(BINS, z.wide), f32(z.parts, LANES), f32(z.parts, LANES)],
+        (positions, energies, w),
+        [f32(z.parts, LANES), f32(z.parts, LANES)],
     )
     return pos_out, ener_out, spectrum
 

time: 73.9 us -> 64.8 us (0.88)
  Pallas kernels: 68.9 us -> 57.9 us
  local copies, waits for them, and re-layouts: 3.1 us -> 5 us
    pallas_call x9, Pallas kernels: 68.9 us -> 57.9 us  [call(): pl.pallas_call(functools.partial(body, z), out_shape=shapes if len(shapes...]
    unnamed x30 -> x26, local copies, waits for them, and re-layouts: 3.08 us -> 4.98 us
where the time goes in v2:
time: 64.8 us; the launch traced here: 64.4 us
  Pallas kernels  57.9 us (89%)
  local copies, waits for them, and re-layouts  5 us (8%)
  between operations  0.81 us (1%)
  other arithmetic  0.73 us (1%)
    pallas_call x9, Pallas kernels, call(): pl.pallas_call(functools.partial(body, z), out_shape=shapes if len(shapes...  57.9 us
    unnamed x26, local copies, waits for them, and re-layouts  4.98 us

profile of v2, /device:TPU:0, one launch (start us, length us, event | category | flops | bytes accessed | tf_op | source)
XLA Modules:
  0.0 64.4 jit_solution(8902202739861277542)
XLA Ops:
  0.6 0.7 %fusion.1 = (s32[704]{0:T(1024)S(1)}, s32[704]{0:T(1024)S(1)}) fusion(s32[704]{0:T(1024)} %param.14), kind=kLoop, calls=%fused_computation.17 | loop fusion | flops 42944 | bytes 8448 | tf_op jit(solution)/shard_map/add | solution.py:97
  1.4 0.0 copy-start.2
  1.4 1.1 %copy-done.2 = f32[704,256]{1,0:T(8,128)S(1)} copy-done((f32[704,256]{1,0:T(8,128)S(1)}, f32[704,256]{1,0:T(8,128)}, u32[]{:S(2)}) %copy-start.2) | copy-done | bytes 720920
  2.5 0.0 copy-start.4
  2.5 0.0 copy-start.8
  2.5 5.1 %shard_map.139.parts = f32[4,8,768]{2,1,0:T(8,128)S(1)} custom-call(f32[704,256]{1,0:T(8,128)S(1)} %copy-done.2), custom_call_target="tpu_custom_call" | custom-call | tf_op jit(solution)/shard_map/pallas_call | solution.py:349
  7.6 12.8 %shard_map.140 = (f32[8,8,768]{2,1,0:T(8,128)S(1)}, s32[8,2,768]{2,1,0:T(2,128)S(1)}) custom-call(f32[4,8,768]{2,1,0:T(8,128)S(1)} %shard_map.139.parts, s32[2,768]{1,0:T(2,128)S(1)} %pad.4.idx), custom_call_target="tpu_custom_call" | custom-call | tf_op jit(solution)/shard_map/pallas_call | solution.py:349
  20.4 0.0 copy-done.4
  20.4 0.0 copy-start
  20.4 1.2 %copy-done = f32[2,16,64,128]{3,2,1,0:T(8,128)S(1)} copy-done((f32[2,16,64,128]{3,2,1,0:T(8,128)S(1)}, f32[2,16,64,128]{3,2,1,0:T(8,128)}, u32[]{:S(2)}) %copy-start) | copy-done | bytes 1048600
  21.6 0.0 copy-start.9
  21.6 0.8 %copy-done.9 = s32[128,1]{1,0:T(8,128)S(1)} copy-done((s32[128,1]{1,0:T(8,128)S(1)}, s32[128,1]{1,0:T(8,128)}, u32[]{:S(2)}) %copy-start.9) | copy-done | bytes 536
  22.5 0.0 copy-start.11
  22.5 0.8 %copy-done.11 = f32[128,64]{1,0:T(8,128)S(1)} copy-done((f32[128,64]{1,0:T(8,128)S(1)}, f32[128,64]{1,0:T(8,128)}, u32[]{:S(2)}) %copy-start.11) | copy-done | bytes 32792
  23.3 2.3 %shard_map.141.parts = f32[4,4,16,128]{3,2,1,0:T(8,128)S(1)} custom-call(f32[8,8,768]{2,1,0:T(8,128)S(1)} %get-tuple-element.9.prof, s32[8,2,768]{2,1,0:T(2,128)S(1)} %get-tuple-element.10.idx, s32[128,1]{1,0:T(8,128)S(1)} %copy-done.9, f32[128,64]{1,0:T(8,128)S(1)} %copy-done.11, f32[2,16,64,128]{3,2,1,0:T(8,128)S(1)} %copy-done, ...), custom_call_target="tpu_custom_call" | custom-call | tf_op jit(solution)/shard_map/pallas_call | solution.py:349
  25.6 6.8 %shard_map.142.y = f32[4,4,16,128]{3,2,1,0:T(8,128)S(1)} custom-call(f32[4,4,16,128]{3,2,1,0:T(8,128)S(1)} %shard_map.141.parts), custom_call_target="tpu_custom_call" | custom-call | tf_op jit(solution)/shard_map/pallas_call | solution.py:349
  32.4 0.0 copy-done.8
  32.4 0.0 copy-done.5
  32.4 0.0 copy-done.6
  32.4 0.0 copy-start.10
  32.4 0.9 %copy-done.10 = f32[2,2,16,4,256]{4,3,2,1,0:T(4,128)S(1)} copy-done((f32[2,2,16,4,256]{4,3,2,1,0:T(4,128)S(1)}, f32[2,2,16,4,256]{4,3,2,1,0:T(4,128)}, u32[]{:S(2)}) %copy-start.10) | copy-done | bytes 262168
  33.4 1.8 %shard_map.143 = (f32[2,16,4,256]{3,2,1,0:T(4,128)}, f32[4,4,16,128]{3,2,1,0:T(8,128)S(1)}) custom-call(f32[4,4,16,128]{3,2,1,0:T(8,128)S(1)} %shard_map.142.y, f32[3,2,16,4,256]{4,3,2,1,0:T(4,128)S(1)} %copy-done.8, f32[2,2,16,4,256]{4,3,2,1,0:T(4,128)S(1)} %copy-done.10, f32[512,512]{1,0:T(8,128)S(1)} %copy-done.6, f32[512,512]{1,0:T(8,128)S(1)} %copy-done.5), custom_call_target="tpu_custom_call" | custom-call | tf_op jit(solution)/shard_map/pallas_call | solution.py:349
  35.1 6.1 %shard_map.144.q = f32[4,4,16,128]{3,2,1,0:T(8,128)S(1)} custom-call(f32[4,4,16,128]{3,2,1,0:T(8,128)S(1)} %get-tuple-element.11.parts), custom_call_target="tpu_custom_call" | custom-call | tf_op jit(solution)/shard_map/pallas_call | solution.py:349
  41.2 0.0 copy-done.1
  41.3 0.0 copy-done.12
  41.3 0.0 copy-start.3
  41.3 0.0 copy-start.7
  41.3 2.1 %shard_map.145.volt = f32[8,8,768]{2,1,0:T(8,128)S(1)} custom-call(f32[4,4,16,128]{3,2,1,0:T(8,128)S(1)} %shard_map.144.q, s32[8,2,768]{2,1,0:T(2,128)S(1)} %get-tuple-element.10.idx, s32[128,1]{1,0:T(8,128)S(1)} %copy-done.9, f32[64,128]{1,0:T(8,128)S(1)} %copy-done.12, f32[2,16,64,128]{3,2,1,0:T(8,128)S(1)} %copy-done.1, f32[2,32,16,128]{3,2,1,0:T(8,128)S(1)} %copy-done.4), custom_call_target="tpu_custom_call" | custom-call | tf_op jit(solution)/shard_map/pallas_call | solution.py:349
  43.4 10.9 %shard_map.146.w = f32[4,8,768]{2,1,0:T(8,128)S(1)} custom-call(f32[8,8,768]{2,1,0:T(8,128)S(1)} %shard_map.145.volt), custom_call_target="tpu_custom_call" | custom-call | tf_op jit(solution)/shard_map/pallas_call | solution.py:349
  54.3 0.0 copy-done.3
  54.3 0.0 copy-done.7
  54.3 10.1 %shard_map.147 = (f32[704,256]{1,0:T(8,128)}, f32[704,256]{1,0:T(8,128)}) custom-call(f32[704,256]{1,0:T(8,128)S(1)} %copy-done.3, f32[704,256]{1,0:T(8,128)S(1)} %copy-done.7, f32[4,8,768]{2,1,0:T(8,128)S(1)} %shard_map.146.w), custom_call_target="tpu_custom_call" | custom-call | tf_op jit(solution)/shard_map/pallas_call | solution.py:349
  (8 shorter events, 0.0 us)
Async XLA Ops:
  1.4 1.1 %copy-start.2 = (f32[704,256]{1,0:T(8,128)S(1)}, f32[704,256]{1,0:T(8,128)}, u32[]{:S(2)}) copy-start(f32[704,256]{1,0:T(8,128)} %pos.3) | copy-start | bytes 2162692
  2.5 17.9 %copy-start.4 = (f32[2,32,16,128]{3,2,1,0:T(8,128)S(1)}, f32[2,32,16,128]{3,2,1,0:T(8,128)}, u32[]{:S(2)}) copy-start(f32[2,32,16,128]{3,2,1,0:T(8,128)} %constant.86.clone.second) | copy-start | bytes 1572868
  2.5 29.9 %copy-start.8 = (f32[3,2,16,4,256]{4,3,2,1,0:T(4,128)S(1)}, f32[3,2,16,4,256]{4,3,2,1,0:T(4,128)}, u32[]{:S(2)}) copy-start(f32[3,2,16,4,256]{4,3,2,1,0:T(4,128)} %imp.1) | copy-start | bytes 1179652
  20.4 1.2 %copy-start = (f32[2,16,64,128]{3,2,1,0:T(8,128)S(1)}, f32[2,16,64,128]{3,2,1,0:T(8,128)}, u32[]{:S(2)}) copy-start(f32[2,16,64,128]{3,2,1,0:T(8,128)} %constant.85.clone.turn) | copy-start | bytes 3145732
  21.6 0.8 %copy-start.9 = (s32[128,1]{1,0:T(8,128)S(1)}, s32[128,1]{1,0:T(8,128)}, u32[]{:S(2)}) copy-start(s32[128,1]{1,0:T(8,128)} %constant.83.clone.lane_key) | copy-start | bytes 1540
  22.5 0.8 %copy-start.11 = (f32[128,64]{1,0:T(8,128)S(1)}, f32[128,64]{1,0:T(8,128)}, u32[]{:S(2)}) copy-start(f32[128,64]{1,0:T(8,128)} %constant.84.clone.first) | copy-start | bytes 98308
  23.3 9.1 %copy-start.5 = (f32[512,512]{1,0:T(8,128)S(1)}, f32[512,512]{1,0:T(8,128)}, u32[]{:S(2)}) copy-start(f32[512,512]{1,0:T(8,128)} %constant.88.clone.back) | copy-start | bytes 3145732
  23.3 9.1 %copy-start.6 = (f32[512,512]{1,0:T(8,128)S(1)}, f32[512,512]{1,0:T(8,128)}, u32[]{:S(2)}) copy-start(f32[512,512]{1,0:T(8,128)} %constant.87.clone.third) | copy-start | bytes 3145732
  32.4 1.0 %copy-start.10 = (f32[2,2,16,4,256]{4,3,2,1,0:T(4,128)S(1)}, f32[2,2,16,4,256]{4,3,2,1,0:T(4,128)}, u32[]{:S(2)}) copy-start(f32[2,2,16,4,256]{4,3,2,1,0:T(4,128)} %hist.1) | copy-start | bytes 786436
  33.4 7.9 %copy-start.1 = (f32[2,16,64,128]{3,2,1,0:T(8,128)S(1)}, f32[2,16,64,128]{3,2,1,0:T(8,128)}, u32[]{:S(2)}) copy-start(f32[2,16,64,128]{3,2,1,0:T(8,128)} %constant.85.clone.turn) | copy-start | bytes 3145732
  35.1 6.1 %copy-start.12 = (f32[64,128]{1,0:T(8,128)S(1)}, f32[64,128]{1,0:T(8,128)}, u32[]{:S(2)}) copy-start(f32[64,128]{1,0:T(8,128)} %constant.89.clone.first_t) | copy-start | bytes 98308
  41.3 13.0 %copy-start.3 = (f32[704,256]{1,0:T(8,128)S(1)}, f32[704,256]{1,0:T(8,128)}, u32[]{:S(2)}) copy-start(f32[704,256]{1,0:T(8,128)} %pos.3) | copy-start | bytes 2162692
  41.3 13.0 %copy-start.7 = (f32[704,256]{1,0:T(8,128)S(1)}, f32[704,256]{1,0:T(8,128)}, u32[]{:S(2)}) copy-start(f32[704,256]{1,0:T(8,128)} %ener.1) | copy-start | bytes 2162692

commit v3 on v2

--- a/solution.py
+++ b/solution.py
@@ -177,12 +177,12 @@
     return copies
 
 
-def forward_comm(z, parts, idx, out, idx_out, slots, total, s0, r0, s1, r1, s2, r2):
-    greet(z, (("dom", z.D), ("grp", z.G)))
+def forward_comm(z, parts, idx, out, idx_out, slots, total, s0, r0, s1, r1, s2, r2, meanwhile):
     copies = push("dom", z.D, lambda to: parts.at[to], lambda me, k: slots.at[k - 1], s0, r0)
     copies_i = push("grp", z.G, lambda to: idx, lambda me, k: idx_out.at[me], s2, r2)
     g = lax.axis_index("grp")
     idx_out[g] = idx[...]
+    meanwhile()
     acc = parts[lax.axis_index("dom")]
     for k, c in enumerate(copies):
         c.wait_recv()
@@ -197,7 +197,6 @@
 
 
 def swap_comm(z, parts, out, send, recv):
-    greet(z, (("dom", z.D),))
     d = lax.axis_index("dom")
     copies = push("dom", z.D, lambda to: parts.at[to], lambda me, k: out.at[me], send, recv)
     out[d] = parts[d]
@@ -206,7 +205,6 @@
 
 
 def backward_comm(z, volt, out, slots, s0, r0, s1, r1):
-    greet(z, (("dom", z.D), ("grp", z.G)))
     copies = push("grp", z.G, lambda to: volt.at[to], lambda me, k: slots.at[k - 1], s0, r0)
     acc = volt[lax.axis_index("grp")]
     for k, c in enumerate(copies):
@@ -250,24 +248,28 @@
         out[:, k] = jnp.where(even, yr, yi).reshape(z.D, z.k1, LANES)
 
 
-def middle_kernel(z, y, imp, hist, third, back, spec, out, volt, cs, sn):
+def phases(z, cs, sn):
     g, d_own = lax.axis_index("grp"), lax.axis_index("dom")
     n = z.k1 * z.k2
     ids = lax.broadcasted_iota(jnp.int32, (n, LANES), 0)
     lane = lax.broadcasted_iota(jnp.int32, (n, LANES), 1)
     freq = d_own * z.k1 + ids % z.k1 + z.n1 * (g * z.k2 + ids // z.k1)
     even = even_lane(z, (n, LANES))
-    total = jnp.zeros((n, 2 * z.n3), jnp.float32)
+    q = lane % z.naq
     for d in range(z.D):
-        q = lane % z.naq
         na = q // z.jb * BINS + q % z.jb + d * z.jb
         ang = (freq * na % z.cycle).astype(jnp.float32)
         ang = ang * (2 * math.pi / z.cycle)
-        c, s = jnp.cos(ang), jnp.sin(ang)
-        s = jnp.where(even, s, -s)
-        cs[d], sn[d] = c, s
+        s = jnp.sin(ang)
+        cs[d], sn[d] = jnp.cos(ang), jnp.where(even, s, -s)
+
+
+def middle_kernel(z, y, imp, hist, third, back, spec, out, volt, cs, sn):
+    n = z.k1 * z.k2
+    total = jnp.zeros((n, 2 * z.n3), jnp.float32)
+    for d in range(z.D):
         p = y[d].reshape(n, LANES)
-        p = p * c + pltpu.roll(p, z.naq, 1) * s
+        p = p * cs[d] + pltpu.roll(p, z.naq, 1) * sn[d]
         total = total + dot3(p, third[d * LANES : (d + 1) * LANES, :])
     for k in range(z.k2):
         rows = slice(k * z.k1, (k + 1) * z.k1)
@@ -312,6 +314,29 @@
     gather(z, volt, idx, lane_key, out)
 
 
+def wake_kernel(
+    z, parts, idx, imp, hist, lane_key, first, first_t, turn, second, third, back, spec, out,
+    prof, idx_all, slots_d, total, x, re, im, y, y_in, mid, cs, sn, q, q_in, volt, rows, slots_g,
+    dom_sems, grp_sems,
+):
+    greet(z, (("dom", z.D), ("grp", z.G)))
+    ds = [dom_sems.at[i] for i in range(8)]
+    gs = [grp_sems.at[i] for i in range(6)]
+    forward_comm(
+        z, parts, idx, prof, idx_all, slots_d, total, ds[0], ds[1], *gs[:4],
+        lambda: phases(z, cs, sn),
+    )
+    forward_kernel(z, prof, idx_all, lane_key, first, turn, second, y, x, re, im)
+    swap_comm(z, y, y_in, ds[2], ds[3])
+    middle_kernel(z, y_in, imp, hist, third, back, spec, q, mid, cs, sn)
+    swap_comm(z, q, q_in, ds[4], ds[5])
+    backward_kernel(
+        z, q_in, idx_all, lane_key, first_t, turn, second, rows, volt,
+        re.at[: z.k2], im.at[: z.k2],
+    )
+    backward_comm(z, rows, out, slots_g, gs[4], gs[5], ds[6], ds[7])
+
+
 def kick_kernel(z, pos, ener, w, pos_out, ener_out, xt, kt):
     step = 64
     for blk in range(z.blocks):
@@ -360,7 +385,6 @@
     z = Sizes(lax.axis_size("grp"), lax.axis_size("dom"), positions, impedance)
     t = tables(z)
     f32 = lambda *s: pltpu.VMEM(s, jnp.float32)
-    dma = lambda n: pltpu.SemaphoreType.DMA((n,))
     row, key = places(z, bucket)
     pad = ((0, 0), (0, z.wide - z.bunches))
     idx = jnp.pad(jnp.stack([row, key]), pad, constant_values=-1)
@@ -369,33 +393,20 @@
     piece = (z.jb, z.wide)
     chunk = (z.D, z.k2, z.k1, LANES)
     parts = call(profile_kernel, z, [(z.D,) + piece], (positions,))
-    prof, idx = call(
-        forward_comm, z,
-        [(z.G,) + piece, jax.ShapeDtypeStruct((z.G,) + idx.shape, jnp.int32)],
-        (parts, idx),
-        [f32(z.D - 1, *piece), f32(*piece), dma(z.D - 1), dma(z.D - 1)] + [dma(z.G - 1)] * 4,
+    n = z.k1 * z.k2
+    spectrum, w = call(
+        wake_kernel, z, [(2, z.k1, z.k2, z.n3), (z.D,) + piece],
+        (parts, idx, impedance, history, lane_key, t["first"], t["first_t"], t["turn"],
+         t["second"], t["third"], t["back"]),
+        [
+            f32(z.G, *piece), pltpu.VMEM((z.G,) + idx.shape, jnp.int32),
+            f32(z.D - 1, *piece), f32(*piece), f32(*full),
+            f32(max(z.mp, z.k2), z.n1, LANES), f32(max(z.mp, z.k2), z.n1, LANES),
+            f32(*chunk), f32(*chunk), f32(n, 2 * z.n3), f32(z.D, n, LANES), f32(z.D, n, LANES),
+            f32(*chunk), f32(*chunk), f32(*full), f32(z.G, *piece), f32(z.G - 1, *piece),
+            pltpu.SemaphoreType.DMA((8, z.D - 1)), pltpu.SemaphoreType.DMA((6, z.G - 1)),
+        ],
         0,
-    )
-    y = call(
-        forward_kernel, z, [chunk], (prof, idx, lane_key, t["first"], t["turn"], t["second"]),
-        [f32(*full), f32(*full), f32(*full)],
-    )
-    y = call(swap_comm, z, [chunk], (y,), [dma(z.D - 1), dma(z.D - 1)], 1)
-    n = z.k1 * z.k2
-    spectrum, q = call(
-        middle_kernel, z, [(2, z.k1, z.k2, z.n3), chunk],
-        (y, impedance, history, t["third"], t["back"]),
-        [f32(n, 2 * z.n3), f32(z.D, n, LANES), f32(z.D, n, LANES)],
-    )
-    q = call(swap_comm, z, [chunk], (q,), [dma(z.D - 1), dma(z.D - 1)], 1)
-    volt = call(
-        backward_kernel, z, [(z.G,) + piece], (q, idx, lane_key, t["first_t"], t["turn"], t["second"]),
-        [f32(*full), f32(z.k2, z.n1, LANES), f32(z.k2, z.n1, LANES)],
-    )
-    w = call(
-        backward_comm, z, [(z.D,) + piece], (volt,),
-        [f32(z.G - 1, *piece), dma(z.G - 1), dma(z.G - 1), dma(z.D - 1), dma(z.D - 1)],
-        2,
     )
     pos_out, ener_out = call(
         kick_kernel, z, [positions.shape, positions.shape],

time: 64.8 us -> 61.2 us (0.944)
  Pallas kernels: 57.9 us -> 51.1 us
  local copies, waits for them, and re-layouts: 5 us -> 8.14 us
    pallas_call x9 -> x3, Pallas kernels: 57.9 us -> 51.1 us  [call(): pl.pallas_call(functools.partial(body, z), out_shape=shapes if len(shapes...]
    unnamed x26 -> x25, local copies, waits for them, and re-layouts: 4.98 us -> 8.12 us
where the time goes in v3:
time: 61.2 us; the launch traced here: 60.7 us
  Pallas kernels  51.1 us (83%)
  local copies, waits for them, and re-layouts  8.14 us (13%)
  other arithmetic  0.73 us (1%)
  between operations  0.73 us (1%)
    pallas_call x3, Pallas kernels, call(): pl.pallas_call(functools.partial(body, z), out_shape=shapes if len(shapes...  51.1 us
    unnamed x25, local copies, waits for them, and re-layouts  8.12 us

profile of v3, /device:TPU:0, one launch (start us, length us, event | category | flops | bytes accessed | tf_op | source)
XLA Modules:
  0.0 60.7 jit_solution(11797428578855352572)
XLA Ops:
  0.6 0.7 %fusion.1 = (s32[704]{0:T(1024)S(1)}, s32[704]{0:T(1024)S(1)}) fusion(s32[704]{0:T(1024)} %param.14), kind=kLoop, calls=%fused_computation.17 | loop fusion | flops 42944 | bytes 8448 | tf_op jit(solution)/shard_map/add | solution.py:97
  1.4 0.0 copy-start
  1.4 1.1 %copy-done = f32[704,256]{1,0:T(8,128)S(1)} copy-done((f32[704,256]{1,0:T(8,128)S(1)}, f32[704,256]{1,0:T(8,128)}, u32[]{:S(2)}) %copy-start) | copy-done | bytes 720920
  2.5 0.0 copy-start.6
  2.5 0.0 copy-start.8
  2.5 0.0 copy-start.11
  2.5 5.1 %shard_map.139.parts = f32[4,8,768]{2,1,0:T(8,128)S(1)} custom-call(f32[704,256]{1,0:T(8,128)S(1)} %copy-done), custom_call_target="tpu_custom_call" | custom-call | tf_op jit(solution)/shard_map/pallas_call | solution.py:374
  7.6 0.0 copy-done.6
  7.6 0.0 copy-done.8
  7.6 0.0 copy-done.11
  7.6 0.0 copy-start.2
  7.6 1.2 %copy-done.2 = f32[512,512]{1,0:T(8,128)S(1)} copy-done((f32[512,512]{1,0:T(8,128)S(1)}, f32[512,512]{1,0:T(8,128)}, u32[]{:S(2)}) %copy-start.2) | copy-done | bytes 1048600
  8.9 0.0 copy-start.3
  8.9 1.2 %copy-done.3 = f32[512,512]{1,0:T(8,128)S(1)} copy-done((f32[512,512]{1,0:T(8,128)S(1)}, f32[512,512]{1,0:T(8,128)}, u32[]{:S(2)}) %copy-start.3) | copy-done | bytes 1048600
  10.1 0.0 copy-start.4
  10.1 1.2 %copy-done.4 = f32[2,16,64,128]{3,2,1,0:T(8,128)S(1)} copy-done((f32[2,16,64,128]{3,2,1,0:T(8,128)S(1)}, f32[2,16,64,128]{3,2,1,0:T(8,128)}, u32[]{:S(2)}) %copy-start.4) | copy-done | bytes 1048600
  11.3 0.0 copy-start.7
  11.3 1.0 %copy-done.7 = f32[3,2,16,4,256]{4,3,2,1,0:T(4,128)S(1)} copy-done((f32[3,2,16,4,256]{4,3,2,1,0:T(4,128)S(1)}, f32[3,2,16,4,256]{4,3,2,1,0:T(4,128)}, u32[]{:S(2)}) %copy-start.7) | copy-done | bytes 393240
  12.3 0.0 copy-start.9
  12.3 0.8 %copy-done.9 = f32[128,64]{1,0:T(8,128)S(1)} copy-done((f32[128,64]{1,0:T(8,128)S(1)}, f32[128,64]{1,0:T(8,128)}, u32[]{:S(2)}) %copy-start.9) | copy-done | bytes 32792
  13.1 0.0 copy-start.10
  13.1 0.8 %copy-done.10 = s32[128,1]{1,0:T(8,128)S(1)} copy-done((s32[128,1]{1,0:T(8,128)S(1)}, s32[128,1]{1,0:T(8,128)}, u32[]{:S(2)}) %copy-start.10) | copy-done | bytes 536
  14.0 0.0 copy-start.1
  14.0 0.0 copy-start.5
  14.0 36.0 %shard_map.140 = (f32[2,16,4,256]{3,2,1,0:T(4,128)S(1)}, f32[4,8,768]{2,1,0:T(8,128)S(1)}) custom-call(f32[4,8,768]{2,1,0:T(8,128)S(1)} %shard_map.139.parts, s32[2,768]{1,0:T(2,128)S(1)} %pad.4.idx, f32[3,2,16,4,256]{4,3,2,1,0:T(4,128)S(1)} %copy-done.7, f32[2,2,16,4,256]{4,3,2,1,0:T(4,128)S(1)} %copy-done.8, s32[128,1]{1,0:T(8,128)S(1)} %copy-done.10, ...), custom_call_target="tpu_custom_call" | custom-call | tf_op jit(solution)/shard_map/pallas_call | solution.py:374
  50.0 0.0 copy-done.1
  50.0 0.0 copy-done.5
  50.0 10.1 %shard_map.141 = (f32[704,256]{1,0:T(8,128)}, f32[704,256]{1,0:T(8,128)}) custom-call(f32[704,256]{1,0:T(8,128)S(1)} %copy-done.1, f32[704,256]{1,0:T(8,128)S(1)} %copy-done.5, f32[4,8,768]{2,1,0:T(8,128)S(1)} %get-tuple-element.7.w), custom_call_target="tpu_custom_call" | custom-call | tf_op jit(solution)/shard_map/pallas_call | solution.py:374
  60.1 0.7 %copy.16 = f32[2,16,4,256]{3,2,1,0:T(4,128)} copy(f32[2,16,4,256]{3,2,1,0:T(4,128)S(1)} %get-tuple-element.18) | data formatting | bytes 262144
  (4 shorter events, 0.0 us)
Async XLA Ops:
  1.4 1.1 %copy-start = (f32[704,256]{1,0:T(8,128)S(1)}, f32[704,256]{1,0:T(8,128)}, u32[]{:S(2)}) copy-start(f32[704,256]{1,0:T(8,128)} %pos.3) | copy-start | bytes 2162692
  2.5 5.1 %copy-start.6 = (f32[2,32,16,128]{3,2,1,0:T(8,128)S(1)}, f32[2,32,16,128]{3,2,1,0:T(8,128)}, u32[]{:S(2)}) copy-start(f32[2,32,16,128]{3,2,1,0:T(8,128)} %constant.87.clone.second) | copy-start | bytes 1572868
  2.5 5.1 %copy-start.8 = (f32[2,2,16,4,256]{4,3,2,1,0:T(4,128)S(1)}, f32[2,2,16,4,256]{4,3,2,1,0:T(4,128)}, u32[]{:S(2)}) copy-start(f32[2,2,16,4,256]{4,3,2,1,0:T(4,128)} %hist.1) | copy-start | bytes 786436
  2.5 5.1 %copy-start.11 = (f32[64,128]{1,0:T(8,128)S(1)}, f32[64,128]{1,0:T(8,128)}, u32[]{:S(2)}) copy-start(f32[64,128]{1,0:T(8,128)} %constant.85.clone.first_t) | copy-start | bytes 98308
  7.6 1.2 %copy-start.2 = (f32[512,512]{1,0:T(8,128)S(1)}, f32[512,512]{1,0:T(8,128)}, u32[]{:S(2)}) copy-start(f32[512,512]{1,0:T(8,128)} %constant.89.clone.back) | copy-start | bytes 3145732
  8.9 1.2 %copy-start.3 = (f32[512,512]{1,0:T(8,128)S(1)}, f32[512,512]{1,0:T(8,128)}, u32[]{:S(2)}) copy-start(f32[512,512]{1,0:T(8,128)} %constant.88.clone.third) | copy-start | bytes 3145732
  10.1 1.2 %copy-start.4 = (f32[2,16,64,128]{3,2,1,0:T(8,128)S(1)}, f32[2,16,64,128]{3,2,1,0:T(8,128)}, u32[]{:S(2)}) copy-start(f32[2,16,64,128]{3,2,1,0:T(8,128)} %constant.86.clone.turn) | copy-start | bytes 3145732
  11.3 1.0 %copy-start.7 = (f32[3,2,16,4,256]{4,3,2,1,0:T(4,128)S(1)}, f32[3,2,16,4,256]{4,3,2,1,0:T(4,128)}, u32[]{:S(2)}) copy-start(f32[3,2,16,4,256]{4,3,2,1,0:T(4,128)} %imp.1) | copy-start | bytes 1179652
  12.3 0.8 %copy-start.9 = (f32[128,64]{1,0:T(8,128)S(1)}, f32[128,64]{1,0:T(8,128)}, u32[]{:S(2)}) copy-start(f32[128,64]{1,0:T(8,128)} %constant.84.clone.first) | copy-start | bytes 98308
  13.1 0.8 %copy-start.10 = (s32[128,1]{1,0:T(8,128)S(1)}, s32[128,1]{1,0:T(8,128)}, u32[]{:S(2)}) copy-start(s32[128,1]{1,0:T(8,128)} %constant.83.clone.lane_key) | copy-start | bytes 1540
  14.0 36.0 %copy-start.1 = (f32[704,256]{1,0:T(8,128)S(1)}, f32[704,256]{1,0:T(8,128)}, u32[]{:S(2)}) copy-start(f32[704,256]{1,0:T(8,128)} %pos.3) | copy-start | bytes 2162692
  14.0 36.0 %copy-start.5 = (f32[704,256]{1,0:T(8,128)S(1)}, f32[704,256]{1,0:T(8,128)}, u32[]{:S(2)}) copy-start(f32[704,256]{1,0:T(8,128)} %ener.1) | copy-start | bytes 2162692
